TPU v7x, 256 devices: a whole 4x4x8 slice. The times are simulated.
256 devices in a mesh: seq: 32 (over x, y, core), ch: 8 (over z).
Axes of the slice: x: 4, y: 4, z: 8, core: 2. Of those that a mesh axis runs over, the one named last changes fastest.
Arguments:
- signal: bfloat16 [128, 16384], P('ch', 'seq'), may hold values from -6 to 6
- cotangent: bfloat16 [128, 16384], P('ch', 'seq'), may hold values from -6 to 6
- filter_taps: float32 [16, 16384], P(None, 'seq'), may hold values from -0.046875 to 0.046875
- skip_gain: float32 [128], P('ch'), may hold values from 0.5 to 1.5
Outputs:
- output: bfloat16 [128, 16384], P('ch', 'seq')
- input_grad: bfloat16 [128, 16384], P('ch', 'seq')
- grad_filter: float32 [16, 16384], P('ch', 'seq')
- grad_skip: float32 [128], replicated
All inputs are finite; a program needn't handle non-finite values.
Results may differ from a plain program's by a relative error of at most 0.0012.
Values sent between devices are 32-bit elements; how exact they have to be, the bound alone decides.
A program may use at most 64 MiB of HBM per device.

v0:
```python
import math

import jax
import jax.numpy as jnp
from jax import lax
from jax.sharding import Mesh
from jax.sharding import PartitionSpec as P

BLOCK = 256
SEQ = ("seq_0", "seq_1", "seq_2")
SEQ_CH = ("seq_0", "seq_1", "seq_2", "ch")


FULL_TURN = 2.0 * math.pi
HIGHEST_PRECISION = lax.Precision.HIGHEST


def in_blocks(shard, dim, peers):
    before, after = (shard.shape[:dim], shard.shape[dim + 1 :])
    return jnp.moveaxis(shard.reshape(*before, peers, -1, *after), dim, 0)


def sent_and_summed(shard, axis, dim):
    pieces = in_blocks(shard, dim, lax.axis_size(axis))
    arrived = lax.all_to_all(pieces, axis, split_axis=0, concat_axis=0, tiled=True)
    return arrived.sum(axis=0)


def one_axis_at_a_time(shard, axes):
    for axis in axes:
        shard = lax.psum(shard, axis)
    return shard


def rotate(values, phase_angle):
    cosine = jnp.cos(phase_angle)
    sine_part = jnp.sin(phase_angle)
    return jnp.stack(
        [values[0] * cosine - values[1] * sine_part, values[0] * sine_part + values[1] * cosine]
    )


def transform(form, values, phase_angle):
    cosine = jnp.cos(phase_angle)
    sine_part = jnp.sin(phase_angle)
    real_part = jnp.einsum(form, values[0], cosine, precision=HIGHEST_PRECISION) - jnp.einsum(
        form, values[1], sine_part, precision=HIGHEST_PRECISION
    )
    imag_part = jnp.einsum(form, values[0], sine_part, precision=HIGHEST_PRECISION) + jnp.einsum(
        form, values[1], cosine, precision=HIGHEST_PRECISION
    )
    return jnp.stack([real_part, imag_part])


def phase_table(left_index, right_index, period, direction):
    product = left_index[:, None] * right_index[None, :] % period
    return direction * FULL_TURN * product.astype(jnp.float32) / period


def multiply(left_side, right_side, conjugate):
    if conjugate:
        real_part = left_side[0] * right_side[0] + left_side[1] * right_side[1]
        imag_part = left_side[0] * right_side[1] - left_side[1] * right_side[0]
    else:
        real_part = left_side[0] * right_side[0] - left_side[1] * right_side[1]
        imag_part = left_side[0] * right_side[1] + left_side[1] * right_side[0]
    return jnp.stack([real_part, imag_part])


def forward_local(values, uprime, total_len):
    local_len = values.shape[3]
    columns = local_len // BLOCK
    positions = jnp.arange(local_len, dtype=jnp.int32)
    indices = 2 * uprime + jnp.arange(2, dtype=jnp.int32)
    values = rotate(values, phase_table(indices, positions, total_len, -1.0))
    shaped = values.reshape(values.shape[:3] + (columns, BLOCK))
    outer_index = jnp.arange(columns, dtype=jnp.int32)
    inner_index = jnp.arange(BLOCK, dtype=jnp.int32)
    shaped = transform(
        "seab,ca->secb", shaped, phase_table(outer_index, outer_index, columns, -1.0)
    )
    shaped = rotate(shaped, phase_table(outer_index, inner_index, local_len, -1.0))
    shaped = transform("seab,cb->seac", shaped, phase_table(inner_index, inner_index, BLOCK, -1.0))
    return shaped.reshape(values.shape)


def inverse_local(values, uprime, total_len):
    local_len = values.shape[3]
    columns = local_len // BLOCK
    positions = jnp.arange(local_len, dtype=jnp.int32)
    indices = 2 * uprime + jnp.arange(2, dtype=jnp.int32)
    outer_index = jnp.arange(columns, dtype=jnp.int32)
    inner_index = jnp.arange(BLOCK, dtype=jnp.int32)
    shaped = values.reshape(values.shape[:3] + (columns, BLOCK))
    shaped = transform("seac,cb->seab", shaped, phase_table(inner_index, inner_index, BLOCK, 1.0))
    shaped = rotate(shaped, phase_table(outer_index, inner_index, local_len, 1.0))
    shaped = transform("secb,ca->seab", shaped, phase_table(outer_index, outer_index, columns, 1.0))
    values = shaped.reshape(values.shape)
    return rotate(values, phase_table(indices, positions, total_len, 1.0))


def forward_transpose(row_block, seq_index, seq_count):
    signals, local_len = row_block.shape
    slice_len = local_len // seq_count
    columns = lax.all_to_all(
        row_block.reshape(signals, seq_count, slice_len),
        SEQ,
        split_axis=1,
        concat_axis=1,
        tiled=True,
    )
    devices = jnp.arange(seq_count, dtype=jnp.int32)
    spectra_index = jnp.arange(2 * seq_count, dtype=jnp.int32)
    phase_angle = phase_table(spectra_index, devices, 2 * seq_count, -1.0)
    real_part = jnp.einsum(
        "up,spk->suk", jnp.cos(phase_angle), columns, precision=HIGHEST_PRECISION
    )
    imag_part = jnp.einsum(
        "up,spk->suk", jnp.sin(phase_angle), columns, precision=HIGHEST_PRECISION
    )
    spectrum = jnp.stack([real_part, imag_part])
    panels = lax.all_to_all(spectrum, SEQ, split_axis=2, concat_axis=3, tiled=True)
    return (panels, seq_index)


def inverse_transpose(values, seq_count, paired_rows):
    local_len = values.shape[3]
    gathered = lax.all_to_all(values, SEQ, split_axis=3, concat_axis=2, tiled=True)
    devices = jnp.arange(seq_count, dtype=jnp.int32)
    spectra_index = jnp.arange(2 * seq_count, dtype=jnp.int32)
    phase_angle = phase_table(devices, spectra_index, 2 * seq_count, 1.0)
    cosine = jnp.cos(phase_angle)
    sine_part = jnp.sin(phase_angle)
    real_part = jnp.einsum(
        "mu,suk->smk", cosine, gathered[0], precision=HIGHEST_PRECISION
    ) - jnp.einsum("mu,suk->smk", sine_part, gathered[1], precision=HIGHEST_PRECISION)
    imag_part = jnp.einsum(
        "mu,suk->smk", cosine, gathered[1, :paired_rows], precision=HIGHEST_PRECISION
    ) + jnp.einsum("mu,suk->smk", sine_part, gathered[0, :paired_rows], precision=HIGHEST_PRECISION)
    combined = jnp.concatenate([real_part, imag_part], axis=0) / (2 * seq_count * local_len)
    returned = lax.all_to_all(combined, SEQ, split_axis=1, concat_axis=2, tiled=True)
    return returned.reshape(combined.shape[0], local_len)


def on_device(signal, cotangent, filter_taps, skip_gain):
    seq_count = lax.axis_size(SEQ)
    seq_index = lax.axis_index(SEQ)
    chan_count = lax.axis_size("ch")
    chan_index = lax.axis_index("ch")
    chan_local, local_len = signal.shape
    filter_count = filter_taps.shape[0]
    seq_total = float(local_len * seq_count)
    total_len = 2 * local_len * seq_count
    signal_f = signal.astype(jnp.float32)
    cot_f = cotangent.astype(jnp.float32)
    row_block = jnp.concatenate([signal_f, cot_f, filter_taps], axis=0)
    panels, uprime = forward_transpose(row_block, seq_index, seq_count)
    spectra = forward_local(panels, uprime, total_len)
    signal_spec = spectra[:, :chan_local]
    cot_spec = spectra[:, chan_local : 2 * chan_local]
    filter_spec = spectra[:, 2 * chan_local :]
    channels = chan_index * chan_local + jnp.arange(chan_local, dtype=jnp.int32)
    selector = (
        channels[:, None] % filter_count == jnp.arange(filter_count, dtype=jnp.int32)[None, :]
    ).astype(jnp.float32)
    chan_filter = jnp.einsum("cf,zfek->zcek", selector, filter_spec, precision=HIGHEST_PRECISION)
    output_spec = multiply(chan_filter, signal_spec, False)
    grad_spec = multiply(chan_filter, cot_spec, True)
    cross_spec = multiply(signal_spec, cot_spec, True)
    filter_grad = jnp.einsum("cf,zcek->zfek", selector, cross_spec, precision=HIGHEST_PRECISION)
    grad_rows = filter_grad.shape[1]
    packed = jnp.stack([output_spec[0] - grad_spec[1], output_spec[1] + grad_spec[0]])
    stacked = jnp.concatenate([packed, filter_grad], axis=1)
    unwound = inverse_local(stacked, uprime, total_len)
    result_rows = inverse_transpose(unwound, seq_count, chan_local)
    conv_out = result_rows[:chan_local]
    lag_grad = result_rows[chan_local : chan_local + grad_rows]
    conv_grad = result_rows[chan_local + grad_rows :]
    lag_grad = sent_and_summed(lag_grad, "ch", 0)
    gain_column = skip_gain[:, None]
    output = (conv_out + gain_column * signal_f).astype(jnp.bfloat16)
    input_grad = (conv_grad + gain_column * cot_f).astype(jnp.bfloat16)
    skip_part = lax.dynamic_update_slice_in_dim(
        jnp.zeros((chan_local * chan_count,), jnp.float32),
        jnp.sum(cot_f * signal_f, axis=1),
        chan_index * chan_local,
        0,
    )
    skip_sum = one_axis_at_a_time(skip_part, SEQ_CH)
    norm_scale = 1.0 / math.sqrt(seq_total)
    return (output, input_grad, lag_grad * norm_scale, skip_sum * norm_scale)


def solution(mesh):
    finer = Mesh(mesh.devices.reshape(4, 4, 2, mesh.shape["ch"]), ("seq_0", "seq_1", "seq_2", "ch"))
    in_specs = (P("ch", SEQ), P("ch", SEQ), P(None, SEQ), P("ch"))
    out_specs = (P("ch", SEQ), P("ch", SEQ), P("ch", SEQ), P())
    return jax.shard_map(
        on_device, mesh=finer, in_specs=in_specs, out_specs=out_specs, check_vma=False
    )
```

profile of v0, /device:TPU:1, one launch (start us, length us, event | category | flops | bytes accessed | tf_op | source)
XLA Modules:
  0.0 141.3 jit_solution(2365181677628859705)
XLA Ops:
  2.3 0.9 reshape.304
  3.1 8.6 %all-to-all-start = ((f32[32,1,768]{2,1,0:T(1,128)}), f32[32,1,768]{2,1,0:T(1,128)S(1)}, u32[]{:S(2)}, u32[]{:S(2)}) async-start(f32[32,1,768]{2,1,0:T(1,128)} %reshape.304), calls=%async_computation | async-start | bytes 196608 | tf_op jit(solution)/shard_map/all_to_all | solution.py:105
  12.0 7.2 %all-to-all-done = f32[32,1,768]{2,1,0:T(1,128)S(1)} async-done(((f32[32,1,768]{2,1,0:T(1,128)}), f32[32,1,768]{2,1,0:T(1,128)S(1)}, u32[]{:S(2)}, u32[]{:S(2)}) %all-to-all-start) | async-done | bytes 98336 | tf_op jit(solution)/shard_map/all_to_all | solution.py:105
  22.5 0.9 copy.133
  23.5 1.7 %reshape.306 = f32[32,1,3072]{2,1,0:T(1,128)} reshape(f32[64,2,16,48]{3,2,1,0:T(8,128)S(1)} %bitcast.154) | data formatting | bytes 786432
  25.2 4.1 %all-to-all-start.1 = ((f32[32,1,3072]{2,1,0:T(1,128)}), f32[32,1,3072]{2,1,0:T(1,128)S(1)}, u32[]{:S(2)}, u32[]{:S(2)}) async-start(f32[32,1,3072]{2,1,0:T(1,128)} %reshape.306), calls=%async_computation.1 | async-start | bytes 786432 | tf_op jit(solution)/shard_map/all_to_all | solution.py:122
  29.6 10.0 %all-to-all-done.1 = f32[32,1,3072]{2,1,0:T(1,128)S(1)} async-done(((f32[32,1,3072]{2,1,0:T(1,128)}), f32[32,1,3072]{2,1,0:T(1,128)S(1)}, u32[]{:S(2)}, u32[]{:S(2)}) %all-to-all-start.1) | async-done | bytes 393248 | tf_op jit(solution)/shard_map/all_to_all | solution.py:122
  39.6 1.6 %reduce.1 = f32[32,3072]{1,0:T(8,128)S(1)} reduce(f32[32,1,3072]{2,1,0:T(1,128)S(1)} %all-to-all-done.1, f32[]{:T(128)} %broadcast.462), dimensions={1}, to_apply=%all_to_all.38.reduce_sub_computation | reduce | bytes 786436 | tf_op jit(solution)/shard_map/all_to_all | solution.py:122
  42.4 1.0 fusion.114
  43.4 1.0 fusion.118
  44.6 1.0 convolution_add_fusion.1
  45.6 1.1 add_bitcast_fusion
  46.8 1.4 fusion.18
  48.2 1.4 fusion.16
  49.5 1.4 convolution_add_fusion
  51.2 1.4 convolution_subtract_fusion.1
  53.9 1.2 fusion.10
  55.1 1.3 fusion.12
  56.5 1.3 convolution_subtract_fusion.3
  57.7 1.3 multiply_add_fusion.2
  62.7 1.0 reshape.308
  63.7 12.3 %all_to_all.52 = f32[32,1,2048]{2,1,0:T(1,128)S(1)} all-to-all(f32[32,1,2048]{2,1,0:T(1,128)S(1)} %reshape.308), channel_id=1, replica_groups=mesh['seq_0'=4,'seq_1'=4,'seq_2'=2,'ch'=8] {'seq_0','seq_1','seq_2'}, dimensions={0} | all-to-all | bytes 524288 | tf_op jit(solution)/shard_map/all_to_all | solution.py:128
  76.0 1.3 reduce.2
  77.3 0.9 reshape.309
  82.5 3.7 %all-to-all-start.3 = ((f32[32,1,768]{2,1,0:T(1,128)}), f32[32,1,768]{2,1,0:T(1,128)S(1)}, u32[]{:S(2)}, u32[]{:S(2)}) async-start(f32[32,1,768]{2,1,0:T(1,128)} %reshape.310), calls=%async_computation.3 | async-start | bytes 196608 | tf_op jit(solution)/shard_map/all_to_all | solution.py:141
  86.2 7.6 %all-to-all-done.3 = f32[32,1,768]{2,1,0:T(1,128)S(1)} async-done(((f32[32,1,768]{2,1,0:T(1,128)}), f32[32,1,768]{2,1,0:T(1,128)S(1)}, u32[]{:S(2)}, u32[]{:S(2)}) %all-to-all-start.3) | async-done | bytes 98336 | tf_op jit(solution)/shard_map/all_to_all | solution.py:141
  93.7 0.9 reduce.3
  96.0 8.2 %all-to-all-start.4 = ((f32[8,2,512]{2,1,0:T(2,128)}), f32[8,2,512]{2,1,0:T(2,128)S(1)}, u32[]{:S(2)}, u32[]{:S(2)}) async-start(f32[8,2,512]{2,1,0:T(2,128)} %reshape.287), calls=%async_computation.4 | async-start | bytes 65536 | tf_op jit(solution)/shard_map/all_to_all | solution.py:25
  106.1 7.1 %psum.28 = f32[128]{0:T(128)S(1)} all-reduce(f32[128]{0:T(128)S(1)} %dynamic_update_slice.3), channel_id=1, replica_groups=mesh['seq_0'=4,'seq_1'=4,'seq_2'=2,'ch'=8] {'seq_0'}, use_global_device_ids=true, to_apply=%region_2.3 | all-reduce | flops 128 | bytes 1024 | tf_op jit(solution)/shard_map/psum | solution.py:31
  113.1 6.9 %psum.29 = f32[128]{0:T(128)S(1)} all-reduce(f32[128]{0:T(128)S(1)} %psum.28), channel_id=1, replica_groups=mesh['seq_0'=4,'seq_1'=4,'seq_2'=2,'ch'=8] {'seq_1'}, use_global_device_ids=true, to_apply=%region_3.4 | all-reduce | flops 128 | bytes 1024 | tf_op jit(solution)/shard_map/psum | solution.py:31
  120.0 6.5 %psum.30 = f32[128]{0:T(128)S(1)} all-reduce(f32[128]{0:T(128)S(1)} %psum.29), channel_id=1, replica_groups=mesh['seq_0'=4,'seq_1'=4,'seq_2'=2,'ch'=8] {'seq_2'}, use_global_device_ids=true, to_apply=%region_4.5 | all-reduce | flops 128 | bytes 1024 | tf_op jit(solution)/shard_map/psum | solution.py:31
  126.6 13.6 %psum.31 = f32[128]{0:T(128)S(1)} all-reduce(f32[128]{0:T(128)S(1)} %psum.30), channel_id=1, replica_groups=mesh['seq_0'=4,'seq_1'=4,'seq_2'=2,'ch'=8] {'ch'}, use_global_device_ids=true, to_apply=%region_5.6 | all-reduce | flops 128 | bytes 1024 | tf_op jit(solution)/shard_map/psum | solution.py:31
  (83 shorter events, 20.5 us)
Async XLA Ops:
  0.6 0.7 copy-start
  1.4 0.8 copy-start.2
  3.1 16.1 %all-to-all-start = ((f32[32,1,768]{2,1,0:T(1,128)}), f32[32,1,768]{2,1,0:T(1,128)S(1)}, u32[]{:S(2)}, u32[]{:S(2)}) async-start(f32[32,1,768]{2,1,0:T(1,128)} %reshape.304), calls=%async_computation | async-start | bytes 196608 | tf_op jit(solution)/shard_map/all_to_all | solution.py:105
  25.2 14.3 %all-to-all-start.1 = ((f32[32,1,3072]{2,1,0:T(1,128)}), f32[32,1,3072]{2,1,0:T(1,128)S(1)}, u32[]{:S(2)}, u32[]{:S(2)}) async-start(f32[32,1,3072]{2,1,0:T(1,128)} %reshape.306), calls=%async_computation.1 | async-start | bytes 786432 | tf_op jit(solution)/shard_map/all_to_all | solution.py:122
  82.5 11.3 %all-to-all-start.3 = ((f32[32,1,768]{2,1,0:T(1,128)}), f32[32,1,768]{2,1,0:T(1,128)S(1)}, u32[]{:S(2)}, u32[]{:S(2)}) async-start(f32[32,1,768]{2,1,0:T(1,128)} %reshape.310), calls=%async_computation.3 | async-start | bytes 196608 | tf_op jit(solution)/shard_map/all_to_all | solution.py:141
  96.0 44.7 %all-to-all-start.4 = ((f32[8,2,512]{2,1,0:T(2,128)}), f32[8,2,512]{2,1,0:T(2,128)S(1)}, u32[]{:S(2)}, u32[]{:S(2)}) async-start(f32[8,2,512]{2,1,0:T(2,128)} %reshape.287), calls=%async_computation.4 | async-start | bytes 65536 | tf_op jit(solution)/shard_map/all_to_all | solution.py:25
  104.3 0.7 copy-start.1
  104.3 0.7 copy-start.3
where the time goes:
time: 144 us; the launch traced here: 141 us
  blocking collectives  46.4 us (32%)
  waiting for transfers between devices  24.8 us (17%)
  starting transfers between devices  24.6 us (17%)
  matrix products  21.2 us (15%)
  local copies, waits for them, and re-layouts  14.8 us (10%)
  other arithmetic  8.39 us (6%)
    psum x4, blocking collectives, one_axis_at_a_time(): shard = lax.psum(shard, axis)  34.1 us
    all_to_all x1, blocking collectives, inverse_transpose(): lax.all_to_all(values, SEQ, split_axis=3, concat_axis=2, tiled=True)  12.3 us
    all_to_all x1, waiting for transfers between devices, forward_transpose(): lax.all_to_all(spectrum, SEQ, split_axis=2, concat_axis=3, tiled=True)  10 us
    all_to_all x1, starting transfers between devices, forward_transpose(): lax.all_to_all(row_block.reshape(signals, seq_count, slice_len), SEQ, spl...  8.59 us
    all_to_all x1, starting transfers between devices, sent_and_summed(): lax.all_to_all(pieces, axis, split_axis=0, concat_axis=0, tiled=True)  8.2 us
    unnamed x18, local copies, waits for them, and re-layouts  8.1 us
    all_to_all x1, waiting for transfers between devices, inverse_transpose(): lax.all_to_all(combined, SEQ, split_axis=1, concat_axis=2, tiled=True)  7.57 us
    all_to_all x1, waiting for transfers between devices, forward_transpose(): lax.all_to_all(row_block.reshape(signals, seq_count, slice_len), SEQ, spl...  7.19 us
  transfers between devices with their start and end apart: 4, of which 3 were waited for; matrix products, arithmetic and copies ran while one was open for 2% of the time, Pallas kernels for 0%

commit v1 on v0

v1 whole, which is shorter than its diff:
```python
import functools
import math

import jax
import jax.numpy as jnp
import ml_dtypes
import numpy as np
from jax import lax
from jax.experimental import pallas as pl
from jax.experimental.pallas import tpu as pltpu
from jax.sharding import PartitionSpec as P

MESH = pl.DeviceIdType.MESH
F32, BF16 = jnp.float32, jnp.bfloat16

CHIPS = 16
PEERS = 32
DEPTH = 8
SIDE = 128
LENGTH = SIDE * SIDE
LOCAL = 512
PIECES = LOCAL // SIDE


def split(table):
    high = table.astype(ml_dtypes.bfloat16)
    low = (table - high.astype(np.float64)).astype(ml_dtypes.bfloat16)
    return high, low


@functools.cache
def tables():
    index = np.arange(SIDE)
    row = np.arange(SIDE)
    position = PIECES * (row % PEERS) + row // PEERS
    turn = 2.0 * np.pi * np.mod(np.outer(4 * index + 1, position), 4 * SIDE) / (4 * SIDE)
    first = np.concatenate([np.cos(turn), -np.sin(turn)], axis=0)
    first_high, first_low = split(first)
    small = 2.0 * np.pi * np.mod(np.outer(index, index), SIDE) / SIDE
    cosine, sine = np.cos(small), np.sin(small)
    middle = np.block([[cosine, -sine], [sine, cosine]])
    last = np.concatenate([np.cos(turn.T), -np.sin(turn.T)], axis=1) / LENGTH
    square = np.concatenate(
        [np.concatenate([first_high, first_low], axis=1), *split(middle), *split(middle.T), *split(last)],
        axis=0,
    )
    angle = 2.0 * np.pi * np.mod(np.outer(4 * index + 1, index), 4 * LENGTH) / (4 * LENGTH)
    twiddle = np.concatenate([np.cos(angle), np.sin(angle)], axis=0).astype(np.float32)
    return square, twiddle


FIRST, MID_H, MID_L, INV_H, INV_L, LAST_H, LAST_L = 0, 256, 512, 768, 1024, 1280, 1408
TABLE_ROWS = 1536


def dot(left, right):
    return jnp.dot(left, right, preferred_element_type=F32)


def halves(value):
    high = value.astype(BF16)
    return high, (value - high.astype(F32)).astype(BF16)


def dot_right(value, table_high, table_low):
    high, low = halves(value)
    return dot(high, table_high) + (dot(low, table_high) + dot(high, table_low))


def dot_left(table_high, table_low, value):
    high, low = halves(value)
    return dot(table_high, high) + (dot(table_high, low) + dot(table_low, high))


def twist(value, twiddle):
    cosine, sine = twiddle[0:SIDE], twiddle[SIDE:]
    real, imag = value[0:SIDE], value[SIDE:]
    return jnp.concatenate([real * cosine + imag * sine, imag * cosine - real * sine], axis=1)


def untwist(value, twiddle):
    cosine, sine = twiddle[0:SIDE], twiddle[SIDE:]
    real, imag = value[:, 0:SIDE], value[:, SIDE:]
    return jnp.concatenate([real * cosine - imag * sine, imag * cosine + real * sine], axis=0)


def forward_exact(value, table, twiddle):
    high = value.astype(BF16)
    columns = dot(table[FIRST : FIRST + 256], jnp.concatenate([high, high], axis=0))
    return twist(columns, twiddle)


def forward_full(value, table, twiddle):
    high, low = halves(value)
    columns = dot(table[FIRST : FIRST + 256], jnp.concatenate([high, high], axis=0))
    columns = columns + dot(table[FIRST : FIRST + 256, 0:SIDE], low)
    return twist(columns, twiddle)


def second(value, table):
    return dot_right(value, table[MID_H : MID_H + 256], table[MID_L : MID_L + 256])


def inverse(spectrum, table, twiddle):
    columns = dot_right(spectrum, table[INV_H : INV_H + 256], table[INV_L : INV_L + 256])
    return dot_left(
        table[LAST_H : LAST_H + SIDE], table[LAST_L : LAST_L + SIDE], untwist(columns, twiddle)
    )


def product(left, right):
    a, b, c, d = left[:, :SIDE], left[:, SIDE:], right[:, :SIDE], right[:, SIDE:]
    return jnp.concatenate([a * c - b * d, a * d + b * c], axis=1)


def product_conj(left, right):
    a, b, c, d = left[:, :SIDE], left[:, SIDE:], right[:, :SIDE], right[:, SIDE:]
    return jnp.concatenate([a * c + b * d, a * d - b * c], axis=1)


def kernel(
    sig_any, cot_any, taps_any, gain_any, table_any, twiddle_any,
    out_ref, grad_ref, lag_ref, skip_ref,
    sig, cot, taps, gain, table, twiddle,
    send_buf, recv_buf, back_buf, home_buf, lag_buf, lag_parts, lag_sum, lag_home, skip_row, skip_parts,
    local_sem, send_sem, recv_sem,
):
    me = lax.axis_index("seq")
    plane = lax.axis_index("ch")
    chip = me // 2
    is_owner = me % 2 == 0

    loads = [
        pltpu.make_async_copy(source, target, local_sem.at[i])
        for i, (source, target) in enumerate(
            ((sig_any, sig), (cot_any, cot), (taps_any, taps), (gain_any, gain), (table_any, table), (twiddle_any, twiddle))
        )
    ]
    for load in loads:
        load.start()

    barrier = pltpu.get_barrier_semaphore()

    def greet(seq, ch):
        pl.semaphore_signal(barrier, inc=1, device_id=(seq, ch), device_id_type=MESH)

    lag_plane = me // 4
    home_plane = chip // 2

    for i in range(1, CHIPS):
        greet(2 * ((chip + i) % CHIPS), plane)
    for j in range(2):
        source = 2 * (2 * plane + j)

        @pl.when(jnp.logical_or(source != me, lag_plane != plane))
        def _():
            greet(source, lag_plane)

    @pl.when(is_owner)
    def _():
        for i in range(CHIPS):
            greet(2 * ((chip + i) % CHIPS) + 1, plane)
        for i in range(1, DEPTH):
            greet(me, (plane + i) % DEPTH)

    @pl.when(jnp.logical_not(is_owner))
    def _():
        greet(me - 1, plane)

    for load in loads[:3]:
        load.wait()
    for r in range(PIECES):
        lanes = slice(SIDE * r, SIDE * (r + 1))
        send_buf[pl.ds(r, CHIPS, stride=16), :] = sig[:, lanes].astype(F32)
        send_buf[pl.ds(PIECES + r, CHIPS, stride=16), :] = cot[:, lanes].astype(F32)
        send_buf[pl.ds(2 * PIECES + r, CHIPS, stride=16), :] = taps[:, lanes]

    def slab(buf, index):
        return buf.at[pl.ds(pl.multiple_of(index * 16, 16), 16)]

    def remote(source, target, which, seq, ch):
        return pltpu.make_async_remote_copy(
            src_ref=source, dst_ref=target, send_sem=send_sem.at[which], recv_sem=recv_sem.at[which],
            device_id=(seq, ch), device_id_type=MESH,
        )

    def send_row(q):
        remote(slab(send_buf, q), slab(recv_buf, me), 0, 2 * q, plane).start()

    def wait_send(buf, slabs, which):
        view = buf.at[pl.ds(0, 16 * slabs)]
        pltpu.make_async_copy(view, view, send_sem.at[which]).wait()

    def wait_recv(buf, slabs, which):
        view = buf.at[pl.ds(0, 16 * slabs)]
        pltpu.make_async_copy(view, view, recv_sem.at[which]).wait()

    lag_self = jnp.logical_and(is_owner, home_plane == plane)

    @pl.when(jnp.logical_not(is_owner))
    def _():
        pl.semaphore_wait(barrier, CHIPS)
        for i in range(CHIPS):
            send_row((chip + i) % CHIPS)
        wait_recv(home_buf, CHIPS, 1)
        wait_send(send_buf, CHIPS, 0)
        for load in loads[3:]:
            load.wait()

    @pl.when(is_owner)
    def _():
        others = jnp.where(home_plane == plane, PIECES - 1, PIECES)
        pl.semaphore_wait(barrier, PEERS - 1 + DEPTH - 1 + others)
        for i in range(1, CHIPS):
            send_row((chip + i) % CHIPS)
        slab(recv_buf, me)[...] = slab(send_buf, chip)[...]
        for load in loads[3:]:
            load.wait()
        wait_recv(recv_buf, PEERS - 1, 0)

        def gather(part):
            return jnp.concatenate(
                [recv_buf[pl.ds(PIECES * part + r, PEERS, stride=16), :] for r in range(PIECES)], axis=0
            )

        signal, cotangent = gather(0), gather(1)
        row = jnp.sum(jnp.sum(signal * cotangent, axis=0, keepdims=True), axis=1, keepdims=True)
        lane = lax.broadcasted_iota(jnp.int32, (8, SIDE), 1)
        skip_row[...] = jnp.where(lane == plane * CHIPS + chip, row, 0.0)
        for i in range(1, DEPTH):
            there = (plane + i) % DEPTH
            remote(skip_row, skip_parts.at[plane], 2, me, there).start()

        signal_spec = second(forward_exact(signal, table, twiddle), table)
        cot_spec = second(forward_exact(cotangent, table, twiddle), table)
        lags = inverse(product_conj(signal_spec, cot_spec), table, twiddle)
        for r in range(PIECES):
            lag_buf[pl.ds(r, PEERS, stride=PIECES), :] = lags[PEERS * r : PEERS * (r + 1)]
        for i in range(1, DEPTH):
            there = (plane + i) % DEPTH
            remote(slab(lag_buf, there), lag_parts.at[plane], 3, me, there).start()
        lag_parts[plane] = slab(lag_buf, plane)[...]

        filter_spec = second(forward_full(gather(2), table, twiddle), table)
        own_gain = gain[chip]
        conv_out = inverse(product(filter_spec, signal_spec), table, twiddle) + own_gain * signal
        conv_grad = inverse(product_conj(filter_spec, cot_spec), table, twiddle) + own_gain * cotangent
        for r in range(PIECES):
            rows = slice(PEERS * r, PEERS * (r + 1))
            back_buf[pl.ds(r, PEERS, stride=16), :] = conv_out[rows]
            back_buf[pl.ds(PIECES + r, PEERS, stride=16), :] = conv_grad[rows]

        skip_view = skip_parts.at[pl.ds(0, DEPTH - 1)]
        pltpu.make_async_copy(skip_view, skip_view, recv_sem.at[2]).wait()
        skip_parts[plane] = skip_row[...]
        skip_all = jnp.sum(skip_parts[...], axis=0)[0:1]
        back_buf[pl.ds(8, PEERS, stride=16), :] = jnp.broadcast_to(skip_all, (PEERS, SIDE))

        for i in range(1, PEERS):
            there = (me + i) % PEERS
            remote(slab(back_buf, there), slab(home_buf, chip), 1, there, plane).start()
        slab(home_buf, chip)[...] = slab(back_buf, me)[...]

        part_view = lag_parts.at[pl.ds(0, DEPTH - 1)]
        pltpu.make_async_copy(part_view, part_view, recv_sem.at[3]).wait()
        total = jnp.sum(lag_parts[...], axis=0) * (1.0 / math.sqrt(LENGTH))
        for j in range(PIECES):
            lag_sum[j, 0:PIECES] = total[PIECES * j : PIECES * (j + 1)]
        for j in range(PIECES):
            there = PIECES * plane + j
            same = jnp.logical_and(there == me, home_plane == plane)

            @pl.when(jnp.logical_not(same))
            def _():
                remote(lag_sum.at[j], lag_home.at[chip % 2], 4 + chip % 2, there, home_plane).start()

            @pl.when(same)
            def _():
                lag_home[chip % 2] = lag_sum[j]

        wait_recv(home_buf, CHIPS - 1, 1)
        wait_send(send_buf, CHIPS - 1, 0)
        wait_send(back_buf, PEERS - 1, 1)
        pltpu.make_async_copy(skip_view, skip_view, send_sem.at[2]).wait()
        pltpu.make_async_copy(part_view, part_view, send_sem.at[3]).wait()

        @pl.when(lag_self)
        def _():
            view = lag_sum.at[pl.ds(0, PIECES - 1)]
            pltpu.make_async_copy(view, view, send_sem.at[4 + chip % 2]).wait()

        @pl.when(jnp.logical_not(lag_self))
        def _():
            pltpu.make_async_copy(lag_sum, lag_sum, send_sem.at[4 + chip % 2]).wait()

    for j in range(2):

        @pl.when(jnp.logical_or(2 * (2 * plane + j) != me, lag_plane != plane))
        def _():
            view = lag_home.at[j]
            pltpu.make_async_copy(view, view, recv_sem.at[4 + j]).wait()

    for r in range(PIECES):
        lanes = slice(SIDE * r, SIDE * (r + 1))
        out_ref[:, lanes] = home_buf[pl.ds(r, CHIPS, stride=16), :].astype(BF16)
        grad_ref[:, lanes] = home_buf[pl.ds(PIECES + r, CHIPS, stride=16), :].astype(BF16)
        for j in range(2):
            lag_ref[j : j + 1, lanes] = lag_home[j, r : r + 1]
    skip_ref[...] = jnp.sum(home_buf[pl.ds(8, CHIPS, stride=16), :], axis=0, keepdims=True) * (1.0 / math.sqrt(LENGTH))


def on_device(signal, cotangent, filter_taps, skip_gain):
    square, twiddle = tables()
    anywhere = pl.BlockSpec(memory_space=pl.ANY)
    vmem = pl.BlockSpec(memory_space=pltpu.VMEM)
    out, grad, lag, skip = pl.pallas_call(
        kernel,
        out_shape=(
            jax.ShapeDtypeStruct((CHIPS, LOCAL), BF16),
            jax.ShapeDtypeStruct((CHIPS, LOCAL), BF16),
            jax.ShapeDtypeStruct((2, LOCAL), F32),
            jax.ShapeDtypeStruct((1, SIDE), F32),
        ),
        in_specs=[anywhere] * 6,
        out_specs=(vmem,) * 4,
        scratch_shapes=[
            pltpu.VMEM((CHIPS, LOCAL), BF16),
            pltpu.VMEM((CHIPS, LOCAL), BF16),
            pltpu.VMEM((CHIPS, LOCAL), F32),
            pltpu.SMEM((CHIPS,), F32),
            pltpu.VMEM((TABLE_ROWS, 2 * SIDE), BF16),
            pltpu.VMEM((2 * SIDE, SIDE), F32),
            pltpu.VMEM((CHIPS * 16, SIDE), F32),
            pltpu.VMEM((PEERS * 16, SIDE), F32),
            pltpu.VMEM((PEERS * 16, SIDE), F32),
            pltpu.VMEM((CHIPS * 16, SIDE), F32),
            pltpu.VMEM((SIDE, SIDE), F32),
            pltpu.VMEM((DEPTH, 16, SIDE), F32),
            pltpu.VMEM((PIECES, 8, SIDE), F32),
            pltpu.VMEM((2, 8, SIDE), F32),
            pltpu.VMEM((8, SIDE), F32),
            pltpu.VMEM((DEPTH, 8, SIDE), F32),
            pltpu.SemaphoreType.DMA((6,)),
            pltpu.SemaphoreType.DMA((6,)),
            pltpu.SemaphoreType.DMA((6,)),
        ],
        compiler_params=pltpu.CompilerParams(
            collective_id=0, has_side_effects=True, vmem_limit_bytes=32 * 1024 * 1024
        ),
    )(signal, cotangent, filter_taps, skip_gain, jnp.asarray(square), jnp.asarray(twiddle))
    return out, grad, lag, skip.reshape(SIDE)


def solution(mesh):
    in_specs = (P("ch", "seq"), P("ch", "seq"), P(None, "seq"), P("ch"))
    out_specs = (P("ch", "seq"), P("ch", "seq"), P("ch", "seq"), P())
    return jax.shard_map(on_device, mesh=mesh, in_specs=in_specs, out_specs=out_specs, check_vma=False)
```

time: 144 us -> 35.4 us (0.25); the launches traced: 141 us -> 35.1 us
  blocking collectives: 46.4 us -> 0 us
  Pallas kernels: 0 us -> 27.2 us
  waiting for transfers between devices: 24.8 us -> 0 us
  starting transfers between devices: 24.6 us -> 0 us
  matrix products: 21.2 us -> 0 us
  other arithmetic: 8.39 us -> 0 us
  local copies, waits for them, and re-layouts: 14.8 us -> 7.19 us
    psum x4 -> x0, blocking collectives: 34.1 us -> none  [one_axis_at_a_time(): shard = lax.psum(shard, axis)]
    pallas_call x0 -> x1, Pallas kernels: none -> 27.2 us  [on_device(): pl.pallas_call(kernel, out_shape=(jax.ShapeDtypeStruct((CHIPS, LOCAL), BF...]
    all_to_all x4 -> x0, waiting for transfers between devices: 24.8 us -> none  [the longest x1 10 us: forward_transpose(): lax.all_to_all(spectrum, SEQ, split_axis=2, concat_axis=3, tiled=True)]
    all_to_all x4 -> x0, starting transfers between devices: 24.6 us -> none  [the longest x1 8.59 us: forward_transpose(): lax.all_to_all(row_block.reshape(signals, seq_count, slice_len), SEQ, spl...]
    dot_general x24 -> x0, matrix products: 21.2 us -> none  [the longest x4 4.39 us: transform(): jnp.einsum(form, values[1], sine_part, precision=HIGHEST_PRECISION)]
    all_to_all x1 -> x0, blocking collectives: 12.3 us -> none  [inverse_transpose(): lax.all_to_all(values, SEQ, split_axis=3, concat_axis=2, tiled=True)]
    all_to_all x4 -> x0, other arithmetic: 4.58 us -> none  [the longest x1 1.57 us: forward_transpose(): lax.all_to_all(spectrum, SEQ, split_axis=2, concat_axis=3, tiled=True)]
    another operation x4 -> x0, local copies, waits for them, and re-layouts: 1.95 us -> none  [the longest x1 0.93 us: forward_transpose(): spectrum = jnp.stack([real_part, imag_part])]
  transfers between devices with their start and end apart: 4 -> 0, of which waited for: 3 -> 0; matrix products, arithmetic and copies ran while one was open for 2% -> 0% of each run, Pallas kernels for 0% -> 0%
where the time goes in v1:
time: 35.4 us; the launch traced here: 35.1 us
  Pallas kernels  27.2 us (77%)
  local copies, waits for them, and re-layouts  7.19 us (20%)
  between operations  0.65 us (2%)
    pallas_call x1, Pallas kernels, on_device(): pl.pallas_call(kernel, out_shape=(jax.ShapeDtypeStruct((CHIPS, LOCAL), BF...  27.2 us
    unnamed x16, local copies, waits for them, and re-layouts  7.19 us

profile of v1, /device:TPU:1, one launch (start us, length us, event | category | flops | bytes accessed | tf_op | source)
XLA Modules:
  0.0 35.1 jit_solution(11880014393901921600)
XLA Ops:
  0.6 0.0 copy-start
  0.6 1.1 %copy-done = bf16[1536,256]{1,0:T(8,128)(2,1)S(1)} copy-done((bf16[1536,256]{1,0:T(8,128)(2,1)S(1)}, bf16[1536,256]{1,0:T(8,128)(2,1)}, u32[]{:S(2)}) %copy-start) | copy-done | bytes 786456
  1.8 0.0 copy-start.1
  1.8 0.9 %copy-done.1 = f32[256,128]{1,0:T(8,128)S(1)} copy-done((f32[256,128]{1,0:T(8,128)S(1)}, f32[256,128]{1,0:T(8,128)}, u32[]{:S(2)}) %copy-start.1) | copy-done | bytes 131096
  2.7 0.0 copy-start.2
  2.7 0.8 %copy-done.2 = f32[16,512]{1,0:T(8,128)S(1)} copy-done((f32[16,512]{1,0:T(8,128)S(1)}, f32[16,512]{1,0:T(8,128)}, u32[]{:S(2)}) %copy-start.2) | copy-done | bytes 32792
  3.4 0.0 copy-start.3
  3.4 0.7 %copy-done.3 = bf16[16,512]{1,0:T(8,128)(2,1)S(1)} copy-done((bf16[16,512]{1,0:T(8,128)(2,1)S(1)}, bf16[16,512]{1,0:T(8,128)(2,1)}, u32[]{:S(2)}) %copy-start.3) | copy-done | bytes 16408
  4.1 0.0 copy-start.4
  4.2 0.7 %copy-done.4 = bf16[16,512]{1,0:T(8,128)(2,1)S(1)} copy-done((bf16[16,512]{1,0:T(8,128)(2,1)S(1)}, bf16[16,512]{1,0:T(8,128)(2,1)}, u32[]{:S(2)}) %copy-start.4) | copy-done | bytes 16408
  4.9 0.0 copy-start.5
  4.9 0.7 %copy-done.5 = f32[16]{0:T(128)S(1)} copy-done((f32[16]{0:T(128)S(1)}, f32[16]{0:T(128)}, u32[]{:S(2)}) %copy-start.5) | copy-done | bytes 88
  5.5 27.2 %shard_map.93 = (bf16[16,512]{1,0:T(8,128)(2,1)S(1)}, bf16[16,512]{1,0:T(8,128)(2,1)S(1)}, f32[2,512]{1,0:T(2,128)S(1)}, f32[1,128]{1,0:T(1,128)S(1)}) custom-call(bf16[16,512]{1,0:T(8,128)(2,1)S(1)} %copy-done.3, bf16[16,512]{1,0:T(8,128)(2,1)S(1)} %copy-done.4, f32[16,512]{1,0:T(8,128)S(1)} %copy-done.2, f32[16]{0:T(128)S(1)} %copy-done.5, ...), custom_call_target="tpu_custom_call" | custom-call | tf_op jit(solution)/shard_map/pallas_call | solution.py:316
  32.8 0.6 %copy.14 = bf16[16,512]{1,0:T(8,128)(2,1)} copy(bf16[16,512]{1,0:T(8,128)(2,1)S(1)} %get-tuple-element.16) | data formatting | bytes 32768
  33.4 0.6 %copy.15 = bf16[16,512]{1,0:T(8,128)(2,1)} copy(bf16[16,512]{1,0:T(8,128)(2,1)S(1)} %get-tuple-element.17) | data formatting | bytes 32768
  34.0 0.6 %copy.16 = f32[2,512]{1,0:T(2,128)} copy(f32[2,512]{1,0:T(2,128)S(1)} %get-tuple-element.18) | data formatting | bytes 8192
  34.6 0.5 %copy.17 = f32[128]{0:T(128)} copy(f32[128]{0:T(128)S(1)} %bitcast.1) | data formatting | bytes 1024
Async XLA Ops:
  0.6 1.1 %copy-start = (bf16[1536,256]{1,0:T(8,128)(2,1)S(1)}, bf16[1536,256]{1,0:T(8,128)(2,1)}, u32[]{:S(2)}) copy-start(bf16[1536,256]{1,0:T(8,128)(2,1)} %constant.4.clone.table_any) | copy-start | bytes 2359300
  1.8 0.9 %copy-start.1 = (f32[256,128]{1,0:T(8,128)S(1)}, f32[256,128]{1,0:T(8,128)}, u32[]{:S(2)}) copy-start(f32[256,128]{1,0:T(8,128)} %constant.5.clone.twiddle_any) | copy-start | bytes 393220
  2.7 0.8 %copy-start.2 = (f32[16,512]{1,0:T(8,128)S(1)}, f32[16,512]{1,0:T(8,128)}, u32[]{:S(2)}) copy-start(f32[16,512]{1,0:T(8,128)} %taps_any.1) | copy-start | bytes 98308
  3.4 0.7 %copy-start.3 = (bf16[16,512]{1,0:T(8,128)(2,1)S(1)}, bf16[16,512]{1,0:T(8,128)(2,1)}, u32[]{:S(2)}) copy-start(bf16[16,512]{1,0:T(8,128)(2,1)} %sig_any.1) | copy-start | bytes 49156
  4.1 0.7 %copy-start.4 = (bf16[16,512]{1,0:T(8,128)(2,1)S(1)}, bf16[16,512]{1,0:T(8,128)(2,1)}, u32[]{:S(2)}) copy-start(bf16[16,512]{1,0:T(8,128)(2,1)} %cot_any.1) | copy-start | bytes 49156
  4.9 0.7 %copy-start.5 = (f32[16]{0:T(128)S(1)}, f32[16]{0:T(128)}, u32[]{:S(2)}) copy-start(f32[16]{0:T(128)} %gain_any.1) | copy-start | bytes 196

commit v2 on v1

v2 whole, which is shorter than its diff:
```python
import functools
import math

import jax
import jax.numpy as jnp
import ml_dtypes
import numpy as np
from jax import lax
from jax.experimental import pallas as pl
from jax.experimental.pallas import tpu as pltpu
from jax.sharding import PartitionSpec as P

MESH = pl.DeviceIdType.MESH
F32, BF16 = jnp.float32, jnp.bfloat16

CHIPS = 16
PEERS = 32
DEPTH = 8
SIDE = 128
LENGTH = SIDE * SIDE
LOCAL = 512
PIECES = LOCAL // SIDE
SCALE = 1.0 / math.sqrt(LENGTH)


def hops(mask):
    return (0, 1, 2, 1)[mask & 3]


CHIP_MASKS = sorted(range(1, CHIPS), key=lambda m: -hops(m) - hops(m >> 2))
DEPTH_STEPS = sorted(range(1, DEPTH), key=lambda i: -min(i, DEPTH - i))


def split(table):
    high = table.astype(ml_dtypes.bfloat16)
    low = (table - high.astype(np.float64)).astype(ml_dtypes.bfloat16)
    return high, low


@functools.cache
def tables():
    index = np.arange(SIDE)
    row = np.arange(SIDE)
    position = PIECES * (row % PEERS) + row // PEERS
    turn = 2.0 * np.pi * np.mod(np.outer(4 * index + 1, position), 4 * SIDE) / (4 * SIDE)
    first = np.concatenate([np.cos(turn), -np.sin(turn)], axis=0)
    first_high, first_low = split(first)
    small = 2.0 * np.pi * np.mod(np.outer(index, index), SIDE) / SIDE
    cosine, sine = np.cos(small), np.sin(small)
    middle = np.block([[cosine, -sine], [sine, cosine]])
    last = np.concatenate([np.cos(turn.T), -np.sin(turn.T)], axis=1) / LENGTH
    square = np.concatenate(
        [np.concatenate([first_high, first_low], axis=1), *split(middle), *split(middle.T), *split(last)],
        axis=0,
    )
    angle = 2.0 * np.pi * np.mod(np.outer(4 * index + 1, index), 4 * LENGTH) / (4 * LENGTH)
    twiddle = np.concatenate([np.cos(angle), np.sin(angle)], axis=0).astype(np.float32)
    return square, twiddle


FIRST, MID_H, MID_L, INV_H, INV_L, LAST_H, LAST_L = 0, 256, 512, 768, 1024, 1280, 1408
TABLE_ROWS = 1536


def dot(left, right):
    return jnp.dot(left, right, preferred_element_type=F32)


def halves(value):
    high = value.astype(BF16)
    return high, (value - high.astype(F32)).astype(BF16)


def dot_right(value, table_high, table_low):
    high, low = halves(value)
    return dot(high, table_high) + (dot(low, table_high) + dot(high, table_low))


def dot_left(table_high, table_low, value):
    high, low = halves(value)
    return dot(table_high, high) + (dot(table_high, low) + dot(table_low, high))


def twist(value, twiddle):
    cosine, sine = twiddle[0:SIDE], twiddle[SIDE:]
    real, imag = value[0:SIDE], value[SIDE:]
    return jnp.concatenate([real * cosine + imag * sine, imag * cosine - real * sine], axis=1)


def untwist(value, twiddle):
    cosine, sine = twiddle[0:SIDE], twiddle[SIDE:]
    real, imag = value[:, 0:SIDE], value[:, SIDE:]
    return jnp.concatenate([real * cosine - imag * sine, imag * cosine + real * sine], axis=0)


def forward_exact(value, table, twiddle):
    high = value.astype(BF16)
    columns = dot(table[FIRST : FIRST + 256], jnp.concatenate([high, high], axis=0))
    return twist(columns, twiddle)


def forward_full(value, table, twiddle):
    high, low = halves(value)
    columns = dot(table[FIRST : FIRST + 256], jnp.concatenate([high, high], axis=0))
    columns = columns + dot(table[FIRST : FIRST + 256, 0:SIDE], low)
    return twist(columns, twiddle)


def second(value, table):
    return dot_right(value, table[MID_H : MID_H + 256], table[MID_L : MID_L + 256])


def inverse(spectrum, table, twiddle):
    columns = dot_right(spectrum, table[INV_H : INV_H + 256], table[INV_L : INV_L + 256])
    return dot_left(
        table[LAST_H : LAST_H + SIDE], table[LAST_L : LAST_L + SIDE], untwist(columns, twiddle)
    )


def product(left, right):
    a, b, c, d = left[:, :SIDE], left[:, SIDE:], right[:, :SIDE], right[:, SIDE:]
    return jnp.concatenate([a * c - b * d, a * d + b * c], axis=1)


def product_conj(left, right):
    a, b, c, d = left[:, :SIDE], left[:, SIDE:], right[:, :SIDE], right[:, SIDE:]
    return jnp.concatenate([a * c + b * d, a * d - b * c], axis=1)


def exchange(
    sig_any, cot_any, taps_any, gain_any, table_any, twiddle_any,
    home_buf, lag_home,
    sig, cot, taps, gain, table, twiddle,
    send_buf, recv_buf, back_buf, lag_buf, skip_row, skip_pair, skip_parts,
    local_sem, send_sem, recv_sem, ready_sem,
):
    me = lax.axis_index("seq")
    plane = lax.axis_index("ch")
    chip = me // 2
    is_owner = me % 2 == 0
    not_owner = jnp.logical_not(is_owner)
    lag_plane = chip // 2
    in_place = lag_plane == plane

    loads = [
        pltpu.make_async_copy(source, target, local_sem.at[i])
        for i, (source, target) in enumerate(
            ((sig_any, sig), (cot_any, cot), (taps_any, taps), (gain_any, gain), (table_any, table), (twiddle_any, twiddle))
        )
    ]
    for load in loads[:3]:
        load.start()

    barrier = pltpu.get_barrier_semaphore()

    def greet(seq, ch):
        pl.semaphore_signal(barrier, inc=1, device_id=(seq, ch), device_id_type=MESH)

    @pl.when(is_owner)
    def _():
        for i in DEPTH_STEPS:
            greet(me, (plane + i) % DEPTH)
        for mask in CHIP_MASKS:
            greet(me ^ (2 * mask), plane)
            greet(me ^ (2 * mask + 1), plane)
        greet(me ^ 1, plane)
        for load in loads[3:]:
            load.start()

    @pl.when(not_owner)
    def _():
        for mask in CHIP_MASKS:
            greet(me ^ (2 * mask + 1), plane)
        greet(me ^ 1, plane)

    for load in loads[:3]:
        load.wait()
    for r in range(PIECES):
        lanes = slice(SIDE * r, SIDE * (r + 1))
        send_buf[pl.ds(r, CHIPS, stride=16), :] = sig[:, lanes].astype(F32)
        send_buf[pl.ds(PIECES + r, CHIPS, stride=16), :] = cot[:, lanes].astype(F32)
        send_buf[pl.ds(2 * PIECES + r, CHIPS, stride=16), :] = taps[:, lanes]
    share = jnp.sum(sig[...].astype(F32) * cot[...].astype(F32), axis=1, keepdims=True)
    lane = lax.broadcasted_iota(jnp.int32, (CHIPS, SIDE), 1)
    local = lax.broadcasted_iota(jnp.int32, (CHIPS, SIDE), 0)
    share = jnp.sum(jnp.where(lane == plane * CHIPS + local, share, 0.0), axis=0, keepdims=True)
    skip_row[...] = jnp.broadcast_to(share, (8, SIDE))

    def slab(buf, index, rows):
        return buf.at[pl.ds(pl.multiple_of(index * 16, 16), rows)]

    def remote(source, target, which, seq, ch):
        return pltpu.make_async_remote_copy(
            src_ref=source, dst_ref=target, send_sem=send_sem.at[which], recv_sem=recv_sem.at[which],
            device_id=(seq, ch), device_id_type=MESH,
        )

    def wait_for(view, sem):
        pltpu.make_async_copy(view, view, sem).wait()

    def send_inputs(mask):
        q = chip ^ mask
        remote(slab(send_buf, q, 16), slab(recv_buf, me, 16), 0, 2 * q, plane).start()

    home_rows = 16

    @pl.when(not_owner)
    def _():
        pl.semaphore_wait(barrier, CHIPS)
        for mask in CHIP_MASKS:
            send_inputs(mask)
        send_inputs(0)
        pair = remote(skip_row, skip_pair, 2, me ^ 1, plane)
        pair.start()
        wait_for(send_buf, send_sem.at[0])
        pair.wait_send()
        wait_for(home_buf, recv_sem.at[1])

    @pl.when(is_owner)
    def _():
        pl.semaphore_wait(barrier, PEERS - 1 + DEPTH - 1)
        for mask in CHIP_MASKS:
            send_inputs(mask)

        @pl.when(in_place)
        def _():
            for i in DEPTH_STEPS:
                pl.semaphore_signal(
                    ready_sem, inc=1, device_id=(me, (plane + i) % DEPTH), device_id_type=MESH
                )

        slab(recv_buf, me, 16)[...] = slab(send_buf, chip, 16)[...]
        remote(skip_row, skip_pair, 2, me, plane).wait_recv()
        skip_row[...] = skip_row[...] + skip_pair[...]
        for i in DEPTH_STEPS:
            remote(skip_row, skip_parts.at[plane], 3, me, (plane + i) % DEPTH).start()
        skip_parts[plane] = skip_row[...]
        for load in loads[3:]:
            load.wait()
        wait_for(recv_buf.at[pl.ds(0, 16 * (PEERS - 1))], recv_sem.at[0])

        def gather(part):
            return jnp.concatenate(
                [recv_buf[pl.ds(PIECES * part + r, PEERS, stride=16), :] for r in range(PIECES)], axis=0
            )

        signal, cotangent = gather(0), gather(1)
        signal_spec = second(forward_exact(signal, table, twiddle), table)
        cot_spec = second(forward_exact(cotangent, table, twiddle), table)
        lags = inverse(product_conj(signal_spec, cot_spec), table, twiddle)
        for r in range(PIECES):
            lag_buf[:, r, :] = lags[PEERS * r : PEERS * (r + 1)]

        @pl.when(jnp.logical_not(in_place))
        def _():
            pl.semaphore_wait(ready_sem, 1)

        slot = (chip % 2) * DEPTH + plane

        def send_lags(mask):
            there = me ^ mask
            return remote(lag_buf.at[there], lag_home.at[slot], 4, there, lag_plane)

        for mask in CHIP_MASKS:
            send_lags(2 * mask).start()
            send_lags(2 * mask + 1).start()
        send_lags(1).start()

        @pl.when(in_place)
        def _():
            pltpu.make_async_copy(lag_buf.at[me], lag_home.at[slot], recv_sem.at[4]).start()

        @pl.when(jnp.logical_not(in_place))
        def _():
            send_lags(0).start()

        filter_spec = second(forward_full(gather(2), table, twiddle), table)
        own_gain = gain[chip]
        conv_out = inverse(product(filter_spec, signal_spec), table, twiddle) + own_gain * signal
        conv_grad = inverse(product_conj(filter_spec, cot_spec), table, twiddle) + own_gain * cotangent
        for r in range(PIECES):
            rows = slice(PEERS * r, PEERS * (r + 1))
            back_buf[pl.ds(r, PEERS, stride=16), :] = conv_out[rows]
            back_buf[pl.ds(PIECES + r, PEERS, stride=16), :] = conv_grad[rows]

        skip_view = skip_parts.at[pl.ds(0, DEPTH - 1)]
        wait_for(skip_view, recv_sem.at[3])
        skip_all = jnp.sum(skip_parts[...], axis=0)[0:1]
        back_buf[pl.ds(8, PEERS, stride=16), :] = jnp.broadcast_to(skip_all, (PEERS, SIDE))

        def send_results(mask):
            there = me ^ mask
            remote(slab(back_buf, there, home_rows), slab(home_buf, chip, home_rows), 1, there, plane).start()

        for mask in CHIP_MASKS:
            send_results(2 * mask)
            send_results(2 * mask + 1)
        send_results(1)
        slab(home_buf, chip, 16)[...] = slab(back_buf, me, 16)[...]

        wait_for(send_buf.at[pl.ds(0, 16 * (CHIPS - 1))], send_sem.at[0])
        wait_for(skip_view, send_sem.at[3])
        wait_for(lag_buf.at[pl.ds(0, PEERS - 1)], send_sem.at[4])

        @pl.when(jnp.logical_not(in_place))
        def _():
            wait_for(lag_buf.at[0], send_sem.at[4])

        wait_for(back_buf.at[pl.ds(0, home_rows * (PEERS - 1))], send_sem.at[1])
        wait_for(home_buf.at[pl.ds(0, home_rows * (CHIPS - 1))], recv_sem.at[1])

    wait_for(lag_home, recv_sem.at[4])


def finish(home_buf, lag_home, out_ref, grad_ref, lag_ref, skip_ref):
    for r in range(PIECES):
        lanes = slice(SIDE * r, SIDE * (r + 1))
        out_ref[:, lanes] = home_buf[pl.ds(r, CHIPS, stride=16), :].astype(BF16)
        grad_ref[:, lanes] = home_buf[pl.ds(PIECES + r, CHIPS, stride=16), :].astype(BF16)
    for j in range(2):
        lags = jnp.sum(lag_home[DEPTH * j : DEPTH * (j + 1)], axis=0) * SCALE
        for r in range(PIECES):
            lag_ref[j : j + 1, SIDE * r : SIDE * (r + 1)] = lags[r : r + 1]
    skip_ref[...] = jnp.sum(home_buf[pl.ds(8, CHIPS, stride=16), :], axis=0) * SCALE


def on_device(signal, cotangent, filter_taps, skip_gain):
    square, twiddle = tables()
    anywhere = pl.BlockSpec(memory_space=pl.ANY)
    vmem = pl.BlockSpec(memory_space=pltpu.VMEM)
    operands = (signal, cotangent, filter_taps, skip_gain, jnp.asarray(square), jnp.asarray(twiddle))
    home, lags = pl.pallas_call(
        exchange,
        out_shape=(
            pltpu.VMEM((CHIPS * 16, SIDE), F32),
            pltpu.VMEM((2 * DEPTH, PIECES, SIDE), F32),
        ),
        in_specs=[anywhere] * 6,
        out_specs=(vmem,) * 2,
        scratch_shapes=[
            pltpu.VMEM((CHIPS, LOCAL), BF16),
            pltpu.VMEM((CHIPS, LOCAL), BF16),
            pltpu.VMEM((CHIPS, LOCAL), F32),
            pltpu.SMEM((CHIPS,), F32),
            pltpu.VMEM((TABLE_ROWS, 2 * SIDE), BF16),
            pltpu.VMEM((2 * SIDE, SIDE), F32),
            pltpu.VMEM((CHIPS * 16, SIDE), F32),
            pltpu.VMEM((PEERS * 16, SIDE), F32),
            pltpu.VMEM((PEERS * 16, SIDE), F32),
            pltpu.VMEM((PEERS, PIECES, SIDE), F32),
            pltpu.VMEM((8, SIDE), F32),
            pltpu.VMEM((8, SIDE), F32),
            pltpu.VMEM((DEPTH, 8, SIDE), F32),
            pltpu.SemaphoreType.DMA((6,)),
            pltpu.SemaphoreType.DMA((5,)),
            pltpu.SemaphoreType.DMA((5,)),
            pltpu.SemaphoreType.REGULAR,
        ],
        compiler_params=pltpu.CompilerParams(
            collective_id=0, has_side_effects=True, vmem_limit_bytes=32 * 1024 * 1024
        ),
        name="exchange",
    )(*(pltpu.with_memory_space_constraint(operand, pltpu.HBM) for operand in operands))
    return pl.pallas_call(
        finish,
        out_shape=(
            jax.ShapeDtypeStruct((CHIPS, LOCAL), BF16),
            jax.ShapeDtypeStruct((CHIPS, LOCAL), BF16),
            jax.ShapeDtypeStruct((2, LOCAL), F32),
            jax.ShapeDtypeStruct((SIDE,), F32),
        ),
        in_specs=[vmem] * 2,
        out_specs=(vmem,) * 4,
        compiler_params=pltpu.CompilerParams(vmem_limit_bytes=8 * 1024 * 1024),
        name="finish",
    )(home, lags)


def solution(mesh):
    in_specs = (P("ch", "seq"), P("ch", "seq"), P(None, "seq"), P("ch"))
    out_specs = (P("ch", "seq"), P("ch", "seq"), P("ch", "seq"), P())
    return jax.shard_map(on_device, mesh=mesh, in_specs=in_specs, out_specs=out_specs, check_vma=False)
```

time: 35.4 us -> 23.8 us (0.67)
  local copies, waits for them, and re-layouts: 7.19 us -> 0 us
  Pallas kernels: 27.2 us -> 23 us
    unnamed x16 -> x0, local copies, waits for them, and re-layouts: 7.19 us -> none
    pallas_call x1 -> x2, Pallas kernels: 27.2 us -> 23 us  [the longest x1 22.4 us: on_device(): pl.pallas_call(exchange, out_shape=(pltpu.VMEM((CHIPS * 16, SIDE), F32),...]
where the time goes in v2:
time: 23.8 us; the launch traced here: 23.6 us
  Pallas kernels  23 us (97%)
  between operations  0.64 us (3%)
    pallas_call x1, Pallas kernels, on_device(): pl.pallas_call(exchange, out_shape=(pltpu.VMEM((CHIPS * 16, SIDE), F32),...  22.4 us
    pallas_call x1, Pallas kernels, on_device(): pl.pallas_call(finish, out_shape=(jax.ShapeDtypeStruct((CHIPS, LOCAL), BF...  0.64 us

profile of v2, /device:TPU:1, one launch (start us, length us, event | category | flops | bytes accessed | tf_op | source)
XLA Modules:
  0.0 23.6 jit_solution(11221150893651132525)
XLA Ops:
  0.6 22.4 %exchange.1 = (f32[256,128]{1,0:T(8,128)S(1)}, f32[16,4,128]{2,1,0:T(4,128)S(1)}) custom-call(bf16[16,512]{1,0:T(8,128)(2,1)} %sig_any.1, bf16[16,512]{1,0:T(8,128)(2,1)} %cot_any.1, f32[16,512]{1,0:T(8,128)} %taps_any.1, f32[16]{0:T(128)} %gain_any.1, bf16[1536,256]{1,0:T(8,128)(2,1)} %constant.4.clone.table_any, f32[256,128]{1,0:T(8,128)} %constant.5.clone.twiddle_any), custom_call_target="tpu_custom_call" | custom-call | tf_op jit(solution)/shard_map/exchange/pallas_call | solution.py:332
  23.0 0.6 %finish.1 = (bf16[16,512]{1,0:T(8,128)(2,1)}, bf16[16,512]{1,0:T(8,128)(2,1)}, f32[2,512]{1,0:T(2,128)}, f32[128]{0:T(128)}) custom-call(f32[256,128]{1,0:T(8,128)S(1)} %get-tuple-element.6.home_buf, f32[16,4,128]{2,1,0:T(4,128)S(1)} %get-tuple-element.7.lag_home), custom_call_target="tpu_custom_call" | custom-call | tf_op jit(solution)/shard_map/finish/pallas_call | solution.py:364

commit v3 on v2

--- a/solution.py
+++ b/solution.py
@@ -19,6 +19,8 @@
 SIDE = 128
 LENGTH = SIDE * SIDE
 LOCAL = 512
+ROWS = 8
+HUB = 1
 PIECES = LOCAL // SIDE
 SCALE = 1.0 / math.sqrt(LENGTH)
 
@@ -129,17 +131,23 @@
 
 def exchange(
     sig_any, cot_any, taps_any, gain_any, table_any, twiddle_any,
-    home_buf, lag_home,
+    home_buf, lag_home, skip_home,
     sig, cot, taps, gain, table, twiddle,
-    send_buf, recv_buf, back_buf, lag_buf, skip_row, skip_pair, skip_parts,
-    local_sem, send_sem, recv_sem, ready_sem,
+    send_buf, send_taps_buf, recv_buf, recv_taps_buf, back_buf, lag_buf, skip_row, skip_in, skip_sum, skip_parts,
+    local_sem, send_sem, recv_sem, plane_sem, ready_sem,
 ):
     me = lax.axis_index("seq")
     plane = lax.axis_index("ch")
     chip = me // 2
     is_owner = me % 2 == 0
-    not_owner = jnp.logical_not(is_owner)
-    lag_plane = chip // 2
+    is_hub = me == HUB
+    shift = (PIECES - (plane & 6)) & 7
+
+    def channel_of(p):
+        return 2 * (((p >> 1) + shift) & 7) + (p & 1)
+
+    channel = channel_of(chip)
+    lag_plane = channel // 2
     in_place = lag_plane == plane
 
     loads = [
@@ -156,38 +164,46 @@
     def greet(seq, ch):
         pl.semaphore_signal(barrier, inc=1, device_id=(seq, ch), device_id_type=MESH)
 
-    @pl.when(is_owner)
-    def _():
-        for i in DEPTH_STEPS:
-            greet(me, (plane + i) % DEPTH)
+    @pl.when(jnp.logical_or(is_owner, is_hub))
+    def _():
         for mask in CHIP_MASKS:
             greet(me ^ (2 * mask), plane)
             greet(me ^ (2 * mask + 1), plane)
         greet(me ^ 1, plane)
+
+    @pl.when(is_hub)
+    def _():
+        for i in DEPTH_STEPS:
+            greet(me, (plane + i) % DEPTH)
+
+    @pl.when(is_owner)
+    def _():
         for load in loads[3:]:
             load.start()
 
-    @pl.when(not_owner)
+    @pl.when(jnp.logical_not(jnp.logical_or(is_owner, is_hub)))
     def _():
         for mask in CHIP_MASKS:
             greet(me ^ (2 * mask + 1), plane)
         greet(me ^ 1, plane)
-
-    for load in loads[:3]:
+        greet(HUB, plane)
+
+    for load in loads[:2]:
         load.wait()
-    for r in range(PIECES):
-        lanes = slice(SIDE * r, SIDE * (r + 1))
-        send_buf[pl.ds(r, CHIPS, stride=16), :] = sig[:, lanes].astype(F32)
-        send_buf[pl.ds(PIECES + r, CHIPS, stride=16), :] = cot[:, lanes].astype(F32)
-        send_buf[pl.ds(2 * PIECES + r, CHIPS, stride=16), :] = taps[:, lanes]
     share = jnp.sum(sig[...].astype(F32) * cot[...].astype(F32), axis=1, keepdims=True)
     lane = lax.broadcasted_iota(jnp.int32, (CHIPS, SIDE), 1)
     local = lax.broadcasted_iota(jnp.int32, (CHIPS, SIDE), 0)
-    share = jnp.sum(jnp.where(lane == plane * CHIPS + local, share, 0.0), axis=0, keepdims=True)
-    skip_row[...] = jnp.broadcast_to(share, (8, SIDE))
-
-    def slab(buf, index, rows):
-        return buf.at[pl.ds(pl.multiple_of(index * 16, 16), rows)]
+    skip_row[...] = jnp.sum(jnp.where(lane == plane * CHIPS + local, share, 0.0), axis=0, keepdims=True)
+    for r in range(PIECES):
+        lanes = slice(SIDE * r, SIDE * (r + 1))
+        send_buf[pl.ds(r, CHIPS, stride=ROWS), :] = sig[:, lanes].astype(F32)
+        send_buf[pl.ds(PIECES + r, CHIPS, stride=ROWS), :] = cot[:, lanes].astype(F32)
+    loads[2].wait()
+    for r in range(PIECES):
+        send_taps_buf[:, r, :] = taps[:, SIDE * r : SIDE * (r + 1)]
+
+    def slab(buf, index):
+        return buf.at[pl.ds(pl.multiple_of(index * ROWS, ROWS), ROWS)]
 
     def remote(source, target, which, seq, ch):
         return pltpu.make_async_remote_copy(
@@ -198,50 +214,89 @@
     def wait_for(view, sem):
         pltpu.make_async_copy(view, view, sem).wait()
 
-    def send_inputs(mask):
+    def send_rows(mask):
         q = chip ^ mask
-        remote(slab(send_buf, q, 16), slab(recv_buf, me, 16), 0, 2 * q, plane).start()
-
-    home_rows = 16
-
-    @pl.when(not_owner)
-    def _():
-        pl.semaphore_wait(barrier, CHIPS)
-        for mask in CHIP_MASKS:
-            send_inputs(mask)
-        send_inputs(0)
-        pair = remote(skip_row, skip_pair, 2, me ^ 1, plane)
-        pair.start()
-        wait_for(send_buf, send_sem.at[0])
-        pair.wait_send()
-        wait_for(home_buf, recv_sem.at[1])
-
-    @pl.when(is_owner)
-    def _():
-        pl.semaphore_wait(barrier, PEERS - 1 + DEPTH - 1)
-        for mask in CHIP_MASKS:
-            send_inputs(mask)
-
-        @pl.when(in_place)
-        def _():
+        remote(slab(send_buf, channel_of(q)), slab(recv_buf, me), 0, 2 * q, plane).start()
+
+    def send_taps(mask):
+        q = chip ^ mask
+        remote(send_taps_buf.at[channel_of(q)], recv_taps_buf.at[me], 5, 2 * q, plane).start()
+
+    def send_share():
+        remote(skip_row, skip_in.at[me], 2, HUB, plane).start()
+
+    def wait_skip():
+        wait_for(skip_row, send_sem.at[2])
+        wait_for(skip_home, recv_sem.at[6])
+
+    @pl.when(jnp.logical_not(is_owner))
+    def _():
+        @pl.when(is_hub)
+        def _():
+            pl.semaphore_wait(barrier, PEERS - 1 + DEPTH - 1)
             for i in DEPTH_STEPS:
                 pl.semaphore_signal(
-                    ready_sem, inc=1, device_id=(me, (plane + i) % DEPTH), device_id_type=MESH
+                    plane_sem, inc=1, device_id=(me, (plane + i) % DEPTH), device_id_type=MESH
                 )
 
-        slab(recv_buf, me, 16)[...] = slab(send_buf, chip, 16)[...]
-        remote(skip_row, skip_pair, 2, me, plane).wait_recv()
-        skip_row[...] = skip_row[...] + skip_pair[...]
-        for i in DEPTH_STEPS:
-            remote(skip_row, skip_parts.at[plane], 3, me, (plane + i) % DEPTH).start()
-        skip_parts[plane] = skip_row[...]
+        @pl.when(jnp.logical_not(is_hub))
+        def _():
+            pl.semaphore_wait(barrier, CHIPS + 1)
+            send_share()
+
+        for mask in (*CHIP_MASKS, 0):
+            send_rows(mask)
+        for mask in (*CHIP_MASKS, 0):
+            send_taps(mask)
+
+        @pl.when(is_hub)
+        def _():
+            pl.semaphore_wait(plane_sem, DEPTH - 1)
+            for mask in (*CHIP_MASKS, 0):
+                pl.semaphore_signal(
+                    ready_sem, inc=1, device_id=(2 * (chip ^ mask), plane), device_id_type=MESH
+                )
+            wait_for(skip_in.at[pl.ds(0, PEERS - 1)], recv_sem.at[2])
+            skip_in[me] = skip_row[...]
+            skip_sum[...] = jnp.sum(skip_in[...], axis=0)
+            for i in DEPTH_STEPS:
+                remote(skip_sum, skip_parts.at[plane], 3, me, (plane + i) % DEPTH).start()
+            others = skip_parts.at[pl.ds(0, DEPTH - 1)]
+            wait_for(others, recv_sem.at[3])
+            skip_parts[plane] = skip_sum[...]
+            skip_home[...] = jnp.sum(skip_parts[...], axis=0)
+            for mask in CHIP_MASKS:
+                remote(skip_home, skip_home, 6, me ^ (2 * mask), plane).start()
+                remote(skip_home, skip_home, 6, me ^ (2 * mask + 1), plane).start()
+            remote(skip_home, skip_home, 6, me ^ 1, plane).start()
+            wait_for(others, send_sem.at[3])
+            wait_for(skip_in.at[pl.ds(0, PEERS - 1)], send_sem.at[6])
+
+        wait_for(send_buf, send_sem.at[0])
+        wait_for(send_taps_buf, send_sem.at[5])
+        wait_for(home_buf, recv_sem.at[1])
+
+        @pl.when(jnp.logical_not(is_hub))
+        def _():
+            wait_skip()
+
+    @pl.when(is_owner)
+    def _():
+        pl.semaphore_wait(barrier, PEERS - 1)
+        send_share()
+        for mask in CHIP_MASKS:
+            send_rows(mask)
+        for mask in CHIP_MASKS:
+            send_taps(mask)
+        slab(recv_buf, me)[...] = slab(send_buf, channel)[...]
+        recv_taps_buf[me] = send_taps_buf[channel]
         for load in loads[3:]:
             load.wait()
-        wait_for(recv_buf.at[pl.ds(0, 16 * (PEERS - 1))], recv_sem.at[0])
+        wait_for(recv_buf.at[pl.ds(0, ROWS * (PEERS - 1))], recv_sem.at[0])
 
         def gather(part):
             return jnp.concatenate(
-                [recv_buf[pl.ds(PIECES * part + r, PEERS, stride=16), :] for r in range(PIECES)], axis=0
+                [recv_buf[pl.ds(PIECES * part + r, PEERS, stride=ROWS), :] for r in range(PIECES)], axis=0
             )
 
         signal, cotangent = gather(0), gather(1)
@@ -251,77 +306,83 @@
         for r in range(PIECES):
             lag_buf[:, r, :] = lags[PEERS * r : PEERS * (r + 1)]
 
-        @pl.when(jnp.logical_not(in_place))
-        def _():
-            pl.semaphore_wait(ready_sem, 1)
-
-        slot = (chip % 2) * DEPTH + plane
+        slot = (channel % 2) * DEPTH + plane
 
         def send_lags(mask):
             there = me ^ mask
             return remote(lag_buf.at[there], lag_home.at[slot], 4, there, lag_plane)
 
-        for mask in CHIP_MASKS:
-            send_lags(2 * mask).start()
-            send_lags(2 * mask + 1).start()
-        send_lags(1).start()
-
-        @pl.when(in_place)
-        def _():
-            pltpu.make_async_copy(lag_buf.at[me], lag_home.at[slot], recv_sem.at[4]).start()
-
-        @pl.when(jnp.logical_not(in_place))
-        def _():
-            send_lags(0).start()
-
-        filter_spec = second(forward_full(gather(2), table, twiddle), table)
-        own_gain = gain[chip]
+        def send_all_lags():
+            pl.semaphore_wait(ready_sem, 1)
+            for mask in CHIP_MASKS:
+                send_lags(2 * mask).start()
+                send_lags(2 * mask + 1).start()
+            send_lags(1).start()
+
+            @pl.when(in_place)
+            def _():
+                pltpu.make_async_copy(lag_buf.at[me], lag_home.at[slot], recv_sem.at[4]).start()
+
+            @pl.when(jnp.logical_not(in_place))
+            def _():
+                send_lags(0).start()
+
+        lags_first = jnp.logical_and(plane >= 3, plane <= 6)
+
+        @pl.when(lags_first)
+        def _():
+            send_all_lags()
+
+        wait_for(recv_taps_buf.at[pl.ds(0, PEERS - 1)], recv_sem.at[5])
+        taps_rows = jnp.concatenate([recv_taps_buf[:, r, :] for r in range(PIECES)], axis=0)
+        filter_spec = second(forward_full(taps_rows, table, twiddle), table)
+        own_gain = gain[channel]
         conv_out = inverse(product(filter_spec, signal_spec), table, twiddle) + own_gain * signal
         conv_grad = inverse(product_conj(filter_spec, cot_spec), table, twiddle) + own_gain * cotangent
         for r in range(PIECES):
             rows = slice(PEERS * r, PEERS * (r + 1))
-            back_buf[pl.ds(r, PEERS, stride=16), :] = conv_out[rows]
-            back_buf[pl.ds(PIECES + r, PEERS, stride=16), :] = conv_grad[rows]
-
-        skip_view = skip_parts.at[pl.ds(0, DEPTH - 1)]
-        wait_for(skip_view, recv_sem.at[3])
-        skip_all = jnp.sum(skip_parts[...], axis=0)[0:1]
-        back_buf[pl.ds(8, PEERS, stride=16), :] = jnp.broadcast_to(skip_all, (PEERS, SIDE))
+            back_buf[pl.ds(r, PEERS, stride=ROWS), :] = conv_out[rows]
+            back_buf[pl.ds(PIECES + r, PEERS, stride=ROWS), :] = conv_grad[rows]
 
         def send_results(mask):
             there = me ^ mask
-            remote(slab(back_buf, there, home_rows), slab(home_buf, chip, home_rows), 1, there, plane).start()
+            remote(slab(back_buf, there), slab(home_buf, channel), 1, there, plane).start()
 
         for mask in CHIP_MASKS:
             send_results(2 * mask)
             send_results(2 * mask + 1)
         send_results(1)
-        slab(home_buf, chip, 16)[...] = slab(back_buf, me, 16)[...]
-
-        wait_for(send_buf.at[pl.ds(0, 16 * (CHIPS - 1))], send_sem.at[0])
-        wait_for(skip_view, send_sem.at[3])
+        slab(home_buf, channel)[...] = slab(back_buf, me)[...]
+
+        @pl.when(jnp.logical_not(lags_first))
+        def _():
+            send_all_lags()
+
+        wait_for(send_buf.at[pl.ds(0, ROWS * (CHIPS - 1))], send_sem.at[0])
+        wait_for(send_taps_buf.at[pl.ds(0, CHIPS - 1)], send_sem.at[5])
+        wait_for(back_buf.at[pl.ds(0, ROWS * (PEERS - 1))], send_sem.at[1])
+        wait_for(home_buf.at[pl.ds(0, ROWS * (CHIPS - 1))], recv_sem.at[1])
         wait_for(lag_buf.at[pl.ds(0, PEERS - 1)], send_sem.at[4])
 
         @pl.when(jnp.logical_not(in_place))
         def _():
             wait_for(lag_buf.at[0], send_sem.at[4])
 
-        wait_for(back_buf.at[pl.ds(0, home_rows * (PEERS - 1))], send_sem.at[1])
-        wait_for(home_buf.at[pl.ds(0, home_rows * (CHIPS - 1))], recv_sem.at[1])
+        wait_skip()
 
     wait_for(lag_home, recv_sem.at[4])
 
 
-def finish(home_buf, lag_home, out_ref, grad_ref, lag_ref, skip_ref):
+def finish(home_buf, lag_home, skip_home, out_ref, grad_ref, lag_ref, skip_ref):
     for r in range(PIECES):
         lanes = slice(SIDE * r, SIDE * (r + 1))
-        out_ref[:, lanes] = home_buf[pl.ds(r, CHIPS, stride=16), :].astype(BF16)
-        grad_ref[:, lanes] = home_buf[pl.ds(PIECES + r, CHIPS, stride=16), :].astype(BF16)
+        out_ref[:, lanes] = home_buf[pl.ds(r, CHIPS, stride=ROWS), :].astype(BF16)
+        grad_ref[:, lanes] = home_buf[pl.ds(PIECES + r, CHIPS, stride=ROWS), :].astype(BF16)
     for j in range(2):
         lags = jnp.sum(lag_home[DEPTH * j : DEPTH * (j + 1)], axis=0) * SCALE
         for r in range(PIECES):
             lag_ref[j : j + 1, SIDE * r : SIDE * (r + 1)] = lags[r : r + 1]
-    skip_ref[...] = jnp.sum(home_buf[pl.ds(8, CHIPS, stride=16), :], axis=0) * SCALE
+    skip_ref[...] = skip_home[0] * SCALE
 
 
 def on_device(signal, cotangent, filter_taps, skip_gain):
@@ -329,14 +390,15 @@
     anywhere = pl.BlockSpec(memory_space=pl.ANY)
     vmem = pl.BlockSpec(memory_space=pltpu.VMEM)
     operands = (signal, cotangent, filter_taps, skip_gain, jnp.asarray(square), jnp.asarray(twiddle))
-    home, lags = pl.pallas_call(
+    received = pl.pallas_call(
         exchange,
         out_shape=(
-            pltpu.VMEM((CHIPS * 16, SIDE), F32),
+            pltpu.VMEM((CHIPS * ROWS, SIDE), F32),
             pltpu.VMEM((2 * DEPTH, PIECES, SIDE), F32),
+            pltpu.VMEM((1, SIDE), F32),
         ),
         in_specs=[anywhere] * 6,
-        out_specs=(vmem,) * 2,
+        out_specs=(vmem,) * 3,
         scratch_shapes=[
             pltpu.VMEM((CHIPS, LOCAL), BF16),
             pltpu.VMEM((CHIPS, LOCAL), BF16),
@@ -344,16 +406,20 @@
             pltpu.SMEM((CHIPS,), F32),
             pltpu.VMEM((TABLE_ROWS, 2 * SIDE), BF16),
             pltpu.VMEM((2 * SIDE, SIDE), F32),
-            pltpu.VMEM((CHIPS * 16, SIDE), F32),
-            pltpu.VMEM((PEERS * 16, SIDE), F32),
-            pltpu.VMEM((PEERS * 16, SIDE), F32),
+            pltpu.VMEM((CHIPS * ROWS, SIDE), F32),
+            pltpu.VMEM((CHIPS, PIECES, SIDE), F32),
+            pltpu.VMEM((PEERS * ROWS, SIDE), F32),
             pltpu.VMEM((PEERS, PIECES, SIDE), F32),
-            pltpu.VMEM((8, SIDE), F32),
-            pltpu.VMEM((8, SIDE), F32),
-            pltpu.VMEM((DEPTH, 8, SIDE), F32),
+            pltpu.VMEM((PEERS * ROWS, SIDE), F32),
+            pltpu.VMEM((PEERS, PIECES, SIDE), F32),
+            pltpu.VMEM((1, SIDE), F32),
+            pltpu.VMEM((PEERS, 1, SIDE), F32),
+            pltpu.VMEM((1, SIDE), F32),
+            pltpu.VMEM((DEPTH, 1, SIDE), F32),
             pltpu.SemaphoreType.DMA((6,)),
-            pltpu.SemaphoreType.DMA((5,)),
-            pltpu.SemaphoreType.DMA((5,)),
+            pltpu.SemaphoreType.DMA((7,)),
+            pltpu.SemaphoreType.DMA((7,)),
+            pltpu.SemaphoreType.REGULAR,
             pltpu.SemaphoreType.REGULAR,
         ],
         compiler_params=pltpu.CompilerParams(
@@ -369,11 +435,11 @@
             jax.ShapeDtypeStruct((2, LOCAL), F32),
             jax.ShapeDtypeStruct((SIDE,), F32),
         ),
-        in_specs=[vmem] * 2,
+        in_specs=[vmem] * 3,
         out_specs=(vmem,) * 4,
         compiler_params=pltpu.CompilerParams(vmem_limit_bytes=8 * 1024 * 1024),
         name="finish",
-    )(home, lags)
+    )(*received)
 
 
 def solution(mesh):

time: 23.8 us -> 23 us (0.966)
  the two profiles are of different devices: /device:TPU:1 before, /device:TPU:97 now
where the time goes in v3:
time: 23 us; the launch traced here: 22.8 us
  Pallas kernels  22.2 us (97%)
  between operations  0.64 us (3%)
    pallas_call x1, Pallas kernels, on_device(): pl.pallas_call(exchange, out_shape=(pltpu.VMEM((CHIPS * ROWS, SIDE), F32)...  21.6 us
    pallas_call x1, Pallas kernels, on_device(): pl.pallas_call(finish, out_shape=(jax.ShapeDtypeStruct((CHIPS, LOCAL), BF...  0.63 us

profile of v3, /device:TPU:97, one launch (start us, length us, event | category | flops | bytes accessed | tf_op | source)
XLA Modules:
  0.0 22.8 jit_solution(12029237657114523023)
XLA Ops:
  0.6 21.6 %exchange.1 = (f32[128,128]{1,0:T(8,128)S(1)}, f32[16,4,128]{2,1,0:T(4,128)S(1)}, f32[1,128]{1,0:T(1,128)S(1)}) custom-call(bf16[16,512]{1,0:T(8,128)(2,1)} %sig_any.1, bf16[16,512]{1,0:T(8,128)(2,1)} %cot_any.1, f32[16,512]{1,0:T(8,128)} %taps_any.1, f32[16]{0:T(128)} %gain_any.1, bf16[1536,256]{1,0:T(8,128)(2,1)} %constant.4.clone.table_any, ...), custom_call_target="tpu_custom_call" | custom-call | tf_op jit(solution)/shard_map/exchange/pallas_call | solution.py:393
  22.2 0.6 %finish.1 = (bf16[16,512]{1,0:T(8,128)(2,1)}, bf16[16,512]{1,0:T(8,128)(2,1)}, f32[2,512]{1,0:T(2,128)}, f32[128]{0:T(128)}) custom-call(f32[128,128]{1,0:T(8,128)S(1)} %get-tuple-element.7.home_buf, f32[16,4,128]{2,1,0:T(4,128)S(1)} %get-tuple-element.8.lag_home, f32[1,128]{1,0:T(1,128)S(1)} %get-tuple-element.9.skip_home), custom_call_target="tpu_custom_call" | custom-call | tf_op jit(solution)/shard_map/finish/pallas_call | solution.py:430

commit v4 on v3

--- a/solution.py
+++ b/solution.py
@@ -149,6 +149,7 @@
     channel = channel_of(chip)
     lag_plane = channel // 2
     in_place = lag_plane == plane
+    lag_half = jnp.where((lag_plane ^ plane) < 4, 0, 1)
 
     loads = [
         pltpu.make_async_copy(source, target, local_sem.at[i])
@@ -235,8 +236,9 @@
         def _():
             pl.semaphore_wait(barrier, PEERS - 1 + DEPTH - 1)
             for i in DEPTH_STEPS:
+                there = (plane + i) % DEPTH
                 pl.semaphore_signal(
-                    plane_sem, inc=1, device_id=(me, (plane + i) % DEPTH), device_id_type=MESH
+                    plane_sem.at[jnp.where((there ^ plane) < 4, 0, 1)], inc=1, device_id=(me, there), device_id_type=MESH
                 )
 
         @pl.when(jnp.logical_not(is_hub))
@@ -251,11 +253,12 @@
 
         @pl.when(is_hub)
         def _():
-            pl.semaphore_wait(plane_sem, DEPTH - 1)
-            for mask in (*CHIP_MASKS, 0):
-                pl.semaphore_signal(
-                    ready_sem, inc=1, device_id=(2 * (chip ^ mask), plane), device_id_type=MESH
-                )
+            for half, planes in ((0, DEPTH // 2 - 1), (1, DEPTH // 2)):
+                pl.semaphore_wait(plane_sem.at[half], planes)
+                for mask in (*CHIP_MASKS, 0):
+                    pl.semaphore_signal(
+                        ready_sem.at[half], inc=1, device_id=(2 * (chip ^ mask), plane), device_id_type=MESH
+                    )
             wait_for(skip_in.at[pl.ds(0, PEERS - 1)], recv_sem.at[2])
             skip_in[me] = skip_row[...]
             skip_sum[...] = jnp.sum(skip_in[...], axis=0)
@@ -313,7 +316,7 @@
             return remote(lag_buf.at[there], lag_home.at[slot], 4, there, lag_plane)
 
         def send_all_lags():
-            pl.semaphore_wait(ready_sem, 1)
+            pl.semaphore_wait(ready_sem.at[lag_half], 1)
             for mask in CHIP_MASKS:
                 send_lags(2 * mask).start()
                 send_lags(2 * mask + 1).start()
@@ -327,7 +330,7 @@
             def _():
                 send_lags(0).start()
 
-        lags_first = jnp.logical_and(plane >= 3, plane <= 6)
+        lags_first = plane >= 2
 
         @pl.when(lags_first)
         def _():
@@ -362,6 +365,7 @@
         wait_for(send_taps_buf.at[pl.ds(0, CHIPS - 1)], send_sem.at[5])
         wait_for(back_buf.at[pl.ds(0, ROWS * (PEERS - 1))], send_sem.at[1])
         wait_for(home_buf.at[pl.ds(0, ROWS * (CHIPS - 1))], recv_sem.at[1])
+        pl.semaphore_wait(ready_sem.at[1 - lag_half], 1)
         wait_for(lag_buf.at[pl.ds(0, PEERS - 1)], send_sem.at[4])
 
         @pl.when(jnp.logical_not(in_place))
@@ -419,8 +423,8 @@
             pltpu.SemaphoreType.DMA((6,)),
             pltpu.SemaphoreType.DMA((7,)),
             pltpu.SemaphoreType.DMA((7,)),
-            pltpu.SemaphoreType.REGULAR,
-            pltpu.SemaphoreType.REGULAR,
+            pltpu.SemaphoreType.REGULAR((2,)),
+            pltpu.SemaphoreType.REGULAR((2,)),
         ],
         compiler_params=pltpu.CompilerParams(
             collective_id=0, has_side_effects=True, vmem_limit_bytes=32 * 1024 * 1024

time: 23 us -> 22.5 us (0.978)
  the two profiles are of different devices: /device:TPU:97 before, /device:TPU:1 now
where the time goes in v4:
time: 22.5 us; the launch traced here: 22.4 us
  Pallas kernels  21.7 us (96%)
  between operations  0.64 us (3%)
    pallas_call x1, Pallas kernels, on_device(): pl.pallas_call(exchange, out_shape=(pltpu.VMEM((CHIPS * ROWS, SIDE), F32)...  21.1 us
    pallas_call x1, Pallas kernels, on_device(): pl.pallas_call(finish, out_shape=(jax.ShapeDtypeStruct((CHIPS, LOCAL), BF...  0.63 us

profile of v4, /device:TPU:1, one launch (start us, length us, event | category | flops | bytes accessed | tf_op | source)
XLA Modules:
  0.0 22.4 jit_solution(15994311449404428766)
XLA Ops:
  0.6 21.1 %exchange.1 = (f32[128,128]{1,0:T(8,128)S(1)}, f32[16,4,128]{2,1,0:T(4,128)S(1)}, f32[1,128]{1,0:T(1,128)S(1)}) custom-call(bf16[16,512]{1,0:T(8,128)(2,1)} %sig_any.1, bf16[16,512]{1,0:T(8,128)(2,1)} %cot_any.1, f32[16,512]{1,0:T(8,128)} %taps_any.1, f32[16]{0:T(128)} %gain_any.1, bf16[1536,256]{1,0:T(8,128)(2,1)} %constant.4.clone.table_any, ...), custom_call_target="tpu_custom_call" | custom-call | tf_op jit(solution)/shard_map/exchange/pallas_call | solution.py:397
  21.7 0.6 %finish.1 = (bf16[16,512]{1,0:T(8,128)(2,1)}, bf16[16,512]{1,0:T(8,128)(2,1)}, f32[2,512]{1,0:T(2,128)}, f32[128]{0:T(128)}) custom-call(f32[128,128]{1,0:T(8,128)S(1)} %get-tuple-element.7.home_buf, f32[16,4,128]{2,1,0:T(4,128)S(1)} %get-tuple-element.8.lag_home, f32[1,128]{1,0:T(1,128)S(1)} %get-tuple-element.9.skip_home), custom_call_target="tpu_custom_call" | custom-call | tf_op jit(solution)/shard_map/finish/pallas_call | solution.py:434

commit v5 on v4

--- a/solution.py
+++ b/solution.py
@@ -311,24 +311,24 @@
 
         slot = (channel % 2) * DEPTH + plane
 
-        def send_lags(mask):
-            there = me ^ mask
+        def send_lags(there):
             return remote(lag_buf.at[there], lag_home.at[slot], 4, there, lag_plane)
 
         def send_all_lags():
             pl.semaphore_wait(ready_sem.at[lag_half], 1)
-            for mask in CHIP_MASKS:
-                send_lags(2 * mask).start()
-                send_lags(2 * mask + 1).start()
-            send_lags(1).start()
-
-            @pl.when(in_place)
-            def _():
-                pltpu.make_async_copy(lag_buf.at[me], lag_home.at[slot], recv_sem.at[4]).start()
-
-            @pl.when(jnp.logical_not(in_place))
-            def _():
-                send_lags(0).start()
+
+            for target in (0, *reversed(CHIP_MASKS)):
+                own = jnp.logical_and(in_place, chip == target)
+
+                @pl.when(jnp.logical_not(own))
+                def _():
+                    send_lags(2 * target).start()
+
+                @pl.when(own)
+                def _():
+                    pltpu.make_async_copy(lag_buf.at[me], lag_home.at[slot], recv_sem.at[4]).start()
+
+                send_lags(2 * target + 1).start()
 
         lags_first = plane >= 2
 

time: 22.5 us -> 22 us (0.978)
  Pallas kernels: 21.7 us -> 21.2 us
    pallas_call x1, Pallas kernels: 21.1 us -> 20.6 us  [on_device(): pl.pallas_call(exchange, out_shape=(pltpu.VMEM((CHIPS * ROWS, SIDE), F32)...]
where the time goes in v5:
time: 22 us; the launch traced here: 21.9 us
  Pallas kernels  21.2 us (96%)
  between operations  0.64 us (3%)
    pallas_call x1, Pallas kernels, on_device(): pl.pallas_call(exchange, out_shape=(pltpu.VMEM((CHIPS * ROWS, SIDE), F32)...  20.6 us
    pallas_call x1, Pallas kernels, on_device(): pl.pallas_call(finish, out_shape=(jax.ShapeDtypeStruct((CHIPS, LOCAL), BF...  0.63 us

profile of v5, /device:TPU:1, one launch (start us, length us, event | category | flops | bytes accessed | tf_op | source)
XLA Modules:
  0.0 21.9 jit_solution(16445035080760031502)
XLA Ops:
  0.6 20.6 %exchange.1 = (f32[128,128]{1,0:T(8,128)S(1)}, f32[16,4,128]{2,1,0:T(4,128)S(1)}, f32[1,128]{1,0:T(1,128)S(1)}) custom-call(bf16[16,512]{1,0:T(8,128)(2,1)} %sig_any.1, bf16[16,512]{1,0:T(8,128)(2,1)} %cot_any.1, f32[16,512]{1,0:T(8,128)} %taps_any.1, f32[16]{0:T(128)} %gain_any.1, bf16[1536,256]{1,0:T(8,128)(2,1)} %constant.4.clone.table_any, ...), custom_call_target="tpu_custom_call" | custom-call | tf_op jit(solution)/shard_map/exchange/pallas_call | solution.py:397
  21.2 0.6 %finish.1 = (bf16[16,512]{1,0:T(8,128)(2,1)}, bf16[16,512]{1,0:T(8,128)(2,1)}, f32[2,512]{1,0:T(2,128)}, f32[128]{0:T(128)}) custom-call(f32[128,128]{1,0:T(8,128)S(1)} %get-tuple-element.7.home_buf, f32[16,4,128]{2,1,0:T(4,128)S(1)} %get-tuple-element.8.lag_home, f32[1,128]{1,0:T(1,128)S(1)} %get-tuple-element.9.skip_home), custom_call_target="tpu_custom_call" | custom-call | tf_op jit(solution)/shard_map/finish/pallas_call | solution.py:434

commit v6 on v5

--- a/solution.py
+++ b/solution.py
@@ -191,17 +191,21 @@
 
     for load in loads[:2]:
         load.wait()
-    share = jnp.sum(sig[...].astype(F32) * cot[...].astype(F32), axis=1, keepdims=True)
-    lane = lax.broadcasted_iota(jnp.int32, (CHIPS, SIDE), 1)
-    local = lax.broadcasted_iota(jnp.int32, (CHIPS, SIDE), 0)
-    skip_row[...] = jnp.sum(jnp.where(lane == plane * CHIPS + local, share, 0.0), axis=0, keepdims=True)
     for r in range(PIECES):
         lanes = slice(SIDE * r, SIDE * (r + 1))
         send_buf[pl.ds(r, CHIPS, stride=ROWS), :] = sig[:, lanes].astype(F32)
         send_buf[pl.ds(PIECES + r, CHIPS, stride=ROWS), :] = cot[:, lanes].astype(F32)
-    loads[2].wait()
-    for r in range(PIECES):
-        send_taps_buf[:, r, :] = taps[:, SIDE * r : SIDE * (r + 1)]
+
+    def stage_taps():
+        loads[2].wait()
+        for r in range(PIECES):
+            send_taps_buf[:, r, :] = taps[:, SIDE * r : SIDE * (r + 1)]
+
+    def form_share():
+        share = jnp.sum(sig[...].astype(F32) * cot[...].astype(F32), axis=1, keepdims=True)
+        lane = lax.broadcasted_iota(jnp.int32, (CHIPS, SIDE), 1)
+        local = lax.broadcasted_iota(jnp.int32, (CHIPS, SIDE), 0)
+        skip_row[...] = jnp.sum(jnp.where(lane == plane * CHIPS + local, share, 0.0), axis=0, keepdims=True)
 
     def slab(buf, index):
         return buf.at[pl.ds(pl.multiple_of(index * ROWS, ROWS), ROWS)]
@@ -244,10 +248,16 @@
         @pl.when(jnp.logical_not(is_hub))
         def _():
             pl.semaphore_wait(barrier, CHIPS + 1)
-            send_share()
 
         for mask in (*CHIP_MASKS, 0):
             send_rows(mask)
+        form_share()
+
+        @pl.when(jnp.logical_not(is_hub))
+        def _():
+            send_share()
+
+        stage_taps()
         for mask in (*CHIP_MASKS, 0):
             send_taps(mask)
 
@@ -286,9 +296,11 @@
     @pl.when(is_owner)
     def _():
         pl.semaphore_wait(barrier, PEERS - 1)
-        send_share()
         for mask in CHIP_MASKS:
             send_rows(mask)
+        form_share()
+        send_share()
+        stage_taps()
         for mask in CHIP_MASKS:
             send_taps(mask)
         slab(recv_buf, me)[...] = slab(send_buf, channel)[...]

time: 22 us -> 22 us (level)
  no operation moved by 1% of the time
where the time goes in v6:
time: 22 us; the launch traced here: 21.9 us
  Pallas kernels  21.2 us (96%)
  between operations  0.64 us (3%)
    pallas_call x1, Pallas kernels, on_device(): pl.pallas_call(exchange, out_shape=(pltpu.VMEM((CHIPS * ROWS, SIDE), F32)...  20.6 us
    pallas_call x1, Pallas kernels, on_device(): pl.pallas_call(finish, out_shape=(jax.ShapeDtypeStruct((CHIPS, LOCAL), BF...  0.63 us

profile of v6, /device:TPU:1, one launch (start us, length us, event | category | flops | bytes accessed | tf_op | source)
XLA Modules:
  0.0 21.9 jit_solution(4409709888321818398)
XLA Ops:
  0.6 20.6 %exchange.1 = (f32[128,128]{1,0:T(8,128)S(1)}, f32[16,4,128]{2,1,0:T(4,128)S(1)}, f32[1,128]{1,0:T(1,128)S(1)}) custom-call(bf16[16,512]{1,0:T(8,128)(2,1)} %sig_any.1, bf16[16,512]{1,0:T(8,128)(2,1)} %cot_any.1, f32[16,512]{1,0:T(8,128)} %taps_any.1, f32[16]{0:T(128)} %gain_any.1, bf16[1536,256]{1,0:T(8,128)(2,1)} %constant.4.clone.table_any, ...), custom_call_target="tpu_custom_call" | custom-call | tf_op jit(solution)/shard_map/exchange/pallas_call | solution.py:409
  21.2 0.6 %finish.1 = (bf16[16,512]{1,0:T(8,128)(2,1)}, bf16[16,512]{1,0:T(8,128)(2,1)}, f32[2,512]{1,0:T(2,128)}, f32[128]{0:T(128)}) custom-call(f32[128,128]{1,0:T(8,128)S(1)} %get-tuple-element.7.home_buf, f32[16,4,128]{2,1,0:T(4,128)S(1)} %get-tuple-element.8.lag_home, f32[1,128]{1,0:T(1,128)S(1)} %get-tuple-element.9.skip_home), custom_call_target="tpu_custom_call" | custom-call | tf_op jit(solution)/shard_map/finish/pallas_call | solution.py:446
